TPU v7x, 32 devices: a whole 2x2x4 slice. The times are simulated.
32 devices in a mesh: hst: 8 (over z, x), doc: 4 (over y, core).
Axes of the slice: x: 2, y: 2, z: 4, core: 2. Of those that a mesh axis runs over, the one named last changes fastest.
Arguments:
- docs: bfloat16 [262144, 768], P(('hst', 'doc')), may hold values from -400 to 400, as said below
- w_in: bfloat16 [768, 256], replicated, may hold values from -0.21875 to 0.21875
- w_out: bfloat16 [256, 64], replicated, may hold values from -0.375 to 0.375
- doc_host: int32 [262144], P(('hst', 'doc')), may hold values from 0 to 2047
- tiles: bfloat16 [2048, 128, 128], P(('hst', 'doc')), may hold values from 0 to 10, as said below
- dst_block: int32 [2048], P(('hst', 'doc')), may hold values from 0 to 15
- src_block: int32 [2048], P(('hst', 'doc')), may hold values from 0 to 127
- tile_count: int32 [32], P(('hst', 'doc')), may hold values from 1 to 64, as said below
- teleport: int32 [16384], P('hst'), may hold values 0 or 1
Outputs:
- scores: float32 [16384, 64], P(('hst', 'doc'))
Inputs may be any that keep to these rules, and one draw needn't show every extreme that they name: `docs`: embeddings stay in the stated range. `tiles`: link weights are nonnegative. `tile_count`: some device uses all 64 slots.
All inputs are finite; a program needn't handle non-finite values. No bound on the sum of `teleport` on one device may be relied on, other than what follows from the above.
Results may differ from a plain program's by a relative error of at most 0.00066.
Values may be sent and summed in bfloat16 or wider, within the bound.
No kernel may reach another device: no remote copies, remote signals or barrier semaphores. Data moves between devices by JAX's collectives and lax.ppermute only.
A program may use at most 128 MiB of HBM per device.

v0:
```python
import functools

import jax
import jax.numpy as jnp
from jax import lax
from jax.experimental import pallas as pl
from jax.experimental.pallas import tpu as pltpu
from jax.sharding import PartitionSpec as P

HOPS = 3
LABELS = 3
DIGITS = 4
DOC_BLOCK = 1024
GROUP = 8
TILE_GROUP = 16
EARLY_TILES = 48
LIFT = 2.0**64
NT = (((1,), (1,)), ((), ()))
MIB = 1 << 20


def xor_send(value, axis, step):
    size = lax.axis_size(axis)
    return lax.ppermute(value, axis, [(i, i ^ step) for i in range(size)])


def column_sum_kernel(source, count, tiles, out, total):
    step = pl.program_id(0)
    parts, rows, _ = out.shape

    @pl.when(step == 0)
    def _():
        total[...] = jnp.zeros_like(total)

    for i in range(GROUP):
        k = step * GROUP + i
        row = jnp.where(k < count[0], source[k], parts * rows)
        part = jnp.sum(tiles[i].astype(jnp.float32), axis=0, keepdims=True)
        total[pl.ds(row, 1), :] += part

    @pl.when(step == pl.num_programs(0) - 1)
    def _():
        for j in range(parts):
            out[j] = total[j * rows : (j + 1) * rows, :]


def column_sums(source, count, tiles, parts, rows):
    slots, block, _ = tiles.shape
    shape = (parts, rows, block)
    return pl.pallas_call(
        column_sum_kernel,
        grid_spec=pltpu.PrefetchScalarGridSpec(
            num_scalar_prefetch=2,
            grid=(slots // GROUP,),
            in_specs=[pl.BlockSpec((GROUP, block, block), lambda i, s, c: (i, 0, 0))],
            out_specs=pl.BlockSpec(shape, lambda i, s, c: (0, 0, 0)),
            scratch_shapes=[pltpu.VMEM((parts * rows + 8, block), jnp.float32)],
        ),
        out_shape=jax.ShapeDtypeStruct(shape, jnp.float32),
        compiler_params=pltpu.CompilerParams(vmem_limit_bytes=56 * MIB),
        cost_estimate=pl.CostEstimate(
            flops=tiles.size, bytes_accessed=tiles.size * 2, transcendentals=0
        ),
        name="column_sums",
    )(source, count, tiles)


def block_topics(docs, w_in, w_out_t, host, width):
    hidden = jax.nn.gelu(
        jnp.dot(docs[...], w_in[...], preferred_element_type=jnp.float32), approximate=True
    ).astype(jnp.bfloat16)
    logits = lax.dot_general(w_out_t[...], hidden, NT, preferred_element_type=jnp.float32)
    powers = jnp.exp(logits - jnp.max(logits, axis=0, keepdims=True))
    probs = powers * (1.0 / jnp.sum(powers, axis=0, keepdims=True))
    high = probs.astype(jnp.bfloat16)
    low = (probs - high.astype(jnp.float32)).astype(jnp.bfloat16)
    index = host[0]
    digit = index // width
    within = index - digit * width
    picks = [jnp.where(digit == j, 1.0, 0.0).astype(jnp.bfloat16) for j in range(DIGITS)]
    left = jnp.concatenate([high * p for p in picks] + [low * p for p in picks], axis=0)
    places = lax.broadcasted_iota(jnp.int32, (width, index.shape[1]), 0)
    right = jnp.where(places == within, 1.0, 0.0).astype(jnp.bfloat16)
    return lax.dot_general(left, right, NT, preferred_element_type=jnp.float32)


def early_documents_kernel(docs, w_in, w_out_t, host, total):
    step = pl.program_id(0)
    added = block_topics(docs, w_in, w_out_t, host, total.shape[1])

    @pl.when(step == 0)
    def _():
        total[...] = added

    @pl.when(step > 0)
    def _():
        total[...] += added


def late_documents_kernel(place, docs, w_in, w_out_t, host, carried, degrees, *rest):
    labels, outs, total = rest[:LABELS], rest[LABELS:-1], rest[-1]
    step = pl.program_id(0)
    topics = w_out_t.shape[0]
    width = total.shape[1]
    added = block_topics(docs, w_in, w_out_t, host, width)

    @pl.when(step == 0)
    def _():
        total[...] = carried[...] + added

    @pl.when(step > 0)
    def _():
        total[...] += added

    @pl.when(step == pl.num_programs(0) - 1)
    def _():
        per = outs[0].shape[0]
        hosts = DIGITS * width
        degree = sum(degrees[j] for j in range(1, degrees.shape[0])) + degrees[0]
        blocks, block = degree.shape
        wide = hosts + blocks // per * block
        for j, out in enumerate(outs):
            chunk = (place[0] ^ j) * per
            for d in range(DIGITS):
                first = pl.ds(pl.multiple_of(d * topics + chunk, 8), per)
                second = pl.ds(pl.multiple_of((DIGITS + d) * topics + chunk, 8), per)
                out[:, d * width : (d + 1) * width] = total[first, :] + total[second, :]
            for c in range(blocks // per):
                cols = slice(hosts + c * block, hosts + (c + 1) * block)
                out[:, cols] = degree[c * per : (c + 1) * per, :]
            out[:, wide:] = jnp.zeros((per, block), jnp.float32)
            for r, label in enumerate(labels):
                out[r : r + 1, wide : wide + label.shape[1]] = label[...].astype(jnp.float32)


def documents(docs, w_in, w_out, doc_host, hosts, split, place, degree_parts, labels, ready):
    count, depth = docs.shape
    hid, topics = w_out.shape
    per = topics // split
    width = hosts // DIGITS
    steps = count // DOC_BLOCK
    half = steps // 2
    host = doc_host.reshape(steps, 1, DOC_BLOCK)
    w_out_t = w_out.T

    def specs(start):
        return [
            pl.BlockSpec((DOC_BLOCK, depth), lambda i, *_: (i + start, 0)),
            pl.BlockSpec((depth, hid), lambda i, *_: (0, 0)),
            pl.BlockSpec((topics, hid), lambda i, *_: (0, 0)),
            pl.BlockSpec((1, 1, DOC_BLOCK), lambda i, *_: (i + start, 0, 0)),
        ]

    def cost(blocks):
        rows = blocks * DOC_BLOCK
        return pl.CostEstimate(
            flops=2 * rows * (depth * hid + hid * topics + 2 * topics * hosts),
            bytes_accessed=rows * depth * 2,
            transcendentals=rows * (hid + topics),
        )

    held = (2 * DIGITS * topics, width)
    carried = pl.pallas_call(
        early_documents_kernel,
        grid=(half,),
        in_specs=specs(0),
        out_specs=pl.BlockSpec(held, lambda i: (0, 0)),
        out_shape=jax.ShapeDtypeStruct(held, jnp.float32),
        compiler_params=pltpu.CompilerParams(vmem_limit_bytes=50 * MIB),
        cost_estimate=cost(half),
        name="early_documents",
    )(docs, w_in, w_out_t, host)
    degrees = lax.all_to_all(degree_parts, "hst", split_axis=0, concat_axis=0, tiled=True)
    degrees, ready = lax.optimization_barrier((degrees, ready))
    shape = (per, hosts + hosts // per + degrees.shape[2])
    sums = pl.pallas_call(
        late_documents_kernel,
        grid_spec=pltpu.PrefetchScalarGridSpec(
            num_scalar_prefetch=1,
            grid=(steps - half,),
            in_specs=specs(half)
            + [
                pl.BlockSpec(held, lambda i, p: (0, 0)),
                pl.BlockSpec(degrees.shape, lambda i, p: (0, 0, 0)),
            ]
            + [pl.BlockSpec(label.shape, lambda i, p: (0, 0)) for label in labels],
            out_specs=[pl.BlockSpec(shape, lambda i, p: (0, 0))] * split,
            scratch_shapes=[pltpu.VMEM(held, jnp.float32)],
        ),
        out_shape=[jax.ShapeDtypeStruct(shape, jnp.float32)] * split,
        compiler_params=pltpu.CompilerParams(vmem_limit_bytes=50 * MIB),
        cost_estimate=cost(steps - half),
        name="late_documents",
    )(place, docs, w_in, w_out_t, host, carried, degrees, *labels)
    return sums, ready


def start_kernel(teleport, *rest):
    sums, (sent, start, inverse, meta) = rest[:-4], rest[-4:]
    per, hosts = start.shape
    blocks, block = teleport.shape
    member = teleport[...].astype(jnp.float32) * LIFT
    mass = jnp.zeros((per, 1), jnp.float32)
    tail = slice(hosts, hosts + inverse.shape[1])
    inv = 1.0 / jnp.maximum(sum(s[:, tail] for s in sums[1:]) + sums[0][:, tail], 1.0)
    inverse[...] = inv
    for j, s in enumerate(sums):
        meta[j * LABELS : (j + 1) * LABELS, :] = s[:LABELS, tail.stop :].astype(jnp.int32)
    for b in range(blocks):
        cols = slice(b * block, (b + 1) * block)
        value = sum(s[:, cols] for s in sums[1:]) + sums[0][:, cols]
        value = value * member[b : b + 1, :]
        start[:, cols] = value
        c, r = b // per, b % per
        row = inv[r : r + 1, c * block : (c + 1) * block]
        sent[:, cols] = (value * row).astype(jnp.bfloat16)
        mass = mass + jnp.sum(value, axis=1, keepdims=True)
    lane = lax.broadcasted_iota(jnp.int32, (per, block), 1)
    first = mass.astype(jnp.bfloat16).astype(jnp.float32)
    second = (mass - first).astype(jnp.bfloat16).astype(jnp.float32)
    third = mass - first - second
    pieces = jnp.where(
        lane == 0, first, jnp.where(lane == 1, second, jnp.where(lane == 2, third, 0.0))
    )
    sent[:, blocks * block :] = pieces.astype(jnp.bfloat16)


def start_values(teleport, sums, block):
    per, _ = sums[0].shape
    hosts = teleport.shape[0]
    vmem = pl.BlockSpec(memory_space=pltpu.VMEM)
    return pl.pallas_call(
        start_kernel,
        in_specs=[vmem] * (1 + len(sums)),
        out_specs=[vmem] * 4,
        out_shape=[
            jax.ShapeDtypeStruct((per, hosts + block), jnp.bfloat16),
            jax.ShapeDtypeStruct((per, hosts), jnp.float32),
            jax.ShapeDtypeStruct((per, hosts // per), jnp.float32),
            jax.ShapeDtypeStruct((len(sums) * LABELS, block), jnp.int32),
        ],
        compiler_params=pltpu.CompilerParams(vmem_limit_bytes=16 * MIB),
        name="start_values",
    )(teleport.reshape(hosts // block, block), *sums)


def hop_kernel(first, last, parts, spans, scale, meta, here, *rest):
    shards, rest = rest[:parts], rest[parts:]
    chunks, rest = rest[: len(spans)], rest[len(spans) :]
    (tele, inverse), outs, (slabs, inflow) = rest[:2], rest[2:-2], rest[-2:]
    blocks, per, block = inflow.shape
    step = pl.program_id(0)

    @pl.when(step == 0)
    def _():
        inflow[...] = jnp.zeros_like(inflow)
        slabs[parts * blocks] = jnp.zeros(slabs.shape[1:], slabs.dtype)
        for j, shard in enumerate(shards):
            for b in range(blocks):
                slabs[j * blocks + b] = shard[:, b * block : (b + 1) * block]

    empty = jnp.zeros((per, block), jnp.bfloat16)
    for tiles, (q, begin, end) in zip(chunks, spans):
        count = meta[q * LABELS + 2, 0]
        within = jnp.logical_and(step >= begin, step < end)

        @pl.when(jnp.logical_and(within, step * TILE_GROUP < count))
        def _():
            products = []
            for c in range(0, TILE_GROUP, 4):
                held = []
                for i in range(4):
                    k = step * TILE_GROUP + c + i
                    source = meta[q * LABELS, k] ^ here[0]
                    held.append(slabs[jnp.where(k < count, source, parts * blocks)])
                left = jnp.concatenate(
                    [
                        jnp.concatenate([held[0], held[1], empty, empty], axis=0),
                        jnp.concatenate([empty, empty, held[2], held[3]], axis=0),
                    ],
                    axis=1,
                )
                right = jnp.concatenate(
                    [
                        tiles[c : c + 2].reshape(2 * block, block),
                        tiles[c + 2 : c + 4].reshape(2 * block, block),
                    ],
                    axis=1,
                )
                both = lax.dot_general(left, right, NT, preferred_element_type=jnp.float32)
                for i in range(4):
                    side = (i % 2) * block
                    products.append(both[i * per : (i + 1) * per, side : side + block])
            for i in range(TILE_GROUP):
                inflow[meta[q * LABELS + 1, step * TILE_GROUP + i]] += products[i]

    @pl.when(step == pl.num_programs(0) - 1)
    def _():
        if first:
            tail = sum(s[:, blocks * block :].astype(jnp.float32) for s in shards)
            mass = jnp.sum(tail, axis=1, keepdims=True)
        for b in range(blocks):
            cols = slice(b * block, (b + 1) * block)
            own = tele[:, cols]
            state = 0.85 * inflow[b] + 0.15 * own
            if first:
                state = state / mass
                outs[1][:, cols] = own / mass
            if last:
                inflow[b] = state * scale
            else:
                c, r = b // per, b % per
                row = inverse[r : r + 1, c * block : (c + 1) * block]
                outs[0][:, cols] = (state * row).astype(jnp.bfloat16)
        if last:
            count = outs[0].shape[1] // block
            for j, out in enumerate(outs):
                begin = (here[1] ^ j) * count
                for i in range(count):
                    out[:, i * block : (i + 1) * block] = inflow[begin + i]


def hop(first, last, meta, here, shards, sets, tele, inverse):
    per, hosts = tele.shape
    slots = sum(chunk.shape[0] for chunk in sets[0])
    block = sets[0][0].shape[1]
    blocks = hosts // block
    parts, split = len(shards), len(sets)
    chunks, spans = [], []
    for q, held in enumerate(sets):
        begin = 0
        for chunk in held:
            end = begin + chunk.shape[0] // TILE_GROUP
            chunks.append(chunk)
            spans.append((q, begin, end))
            begin = end

    def stream(span):
        _, begin, end = span
        return pl.BlockSpec(
            (TILE_GROUP, block, block),
            lambda i, m, p: (jnp.clip(i - begin, 0, end - begin - 1), 0, 0),
        )

    if last:
        out_shape = [jax.ShapeDtypeStruct((per, hosts // split), jnp.float32)] * split
    else:
        out_shape = [jax.ShapeDtypeStruct((per, hosts), jnp.bfloat16)]
        if first:
            out_shape.append(jax.ShapeDtypeStruct((per, hosts), jnp.float32))

    def whole(array):
        return pl.BlockSpec(array.shape, lambda i, m, p: (0,) * len(array.shape))

    return pl.pallas_call(
        functools.partial(hop_kernel, first, last, parts, spans, float(parts * hosts)),
        grid_spec=pltpu.PrefetchScalarGridSpec(
            num_scalar_prefetch=2,
            grid=(slots // TILE_GROUP,),
            in_specs=[whole(s) for s in shards]
            + [stream(span) for span in spans]
            + [whole(tele), whole(inverse)],
            out_specs=[whole(s) for s in out_shape],
            scratch_shapes=[
                pltpu.VMEM((parts * blocks + 1, per, block), jnp.bfloat16),
                pltpu.VMEM((blocks, per, block), jnp.float32),
            ],
        ),
        out_shape=out_shape,
        compiler_params=pltpu.CompilerParams(vmem_limit_bytes=16 * MIB),
        cost_estimate=pl.CostEstimate(
            flops=2 * split * slots * block * block * per,
            bytes_accessed=split * slots * block * block * 2,
            transcendentals=0,
        ),
        name="hop",
    )(meta, here, *shards, *chunks, tele, inverse)


def finish_kernel(here, *rest):
    chunks, out = rest[:-1], rest[-1]
    per = chunks[0].shape[0]
    for j, chunk in enumerate(chunks):
        out[pl.ds(pl.multiple_of((here[1] ^ j) * per, 8), per), :] = chunk[...]


def finish(here, chunks):
    per, rows = chunks[0].shape
    topics = per * len(chunks)
    return pl.pallas_call(
        finish_kernel,
        in_specs=[pl.BlockSpec(memory_space=pltpu.SMEM)]
        + [pl.BlockSpec(memory_space=pltpu.VMEM)] * len(chunks),
        out_shape=jax.ShapeDtypeStruct((topics, rows), jnp.float32),
        compiler_params=pltpu.CompilerParams(vmem_limit_bytes=16 * MIB),
        name="finish",
    )(here, *chunks)


def spread(sent, axis):
    held = {0: sent}
    for j in range(2, lax.axis_size(axis), 2):
        held[j] = xor_send(sent, axis, j)
    for j in range(0, lax.axis_size(axis), 2):
        held[j + 1] = xor_send(held[j], axis, 1)
    return [held[j] for j in range(len(held))]


def body(docs, w_in, w_out, doc_host, tiles, dst_block, src_block, tile_count, teleport):
    hosts = teleport.shape[0]
    slots, block, _ = tiles.shape
    parts, split = lax.axis_size("hst"), lax.axis_size("doc")
    blocks = hosts // block
    place = lax.axis_index("doc").astype(jnp.int32)
    here = jnp.stack([lax.axis_index("hst").astype(jnp.int32) * blocks, place])
    labels = [label.reshape(1, -1) for label in (src_block, dst_block, tile_count)]

    near = xor_send(tiles, "doc", 1)
    cut = slots * EARLY_TILES // 64
    early, late = tiles[:cut], tiles[cut:]
    far = {j: [xor_send(early, "doc", j)] for j in range(2, split, 2)}
    degree_parts = column_sums(src_block, tile_count, tiles, parts, blocks)
    sums, near = documents(
        docs, w_in, w_out, doc_host, hosts, split, place.reshape(1), degree_parts, labels, near
    )
    sums = [sums[0]] + [xor_send(sums[j], "doc", j) for j in range(1, split)]
    sums, late, far = lax.optimization_barrier((sums, late, far))
    for j in range(2, split, 2):
        far[j].append(xor_send(late, "doc", j))
        far[j + 1] = [xor_send(far[j][0], "doc", 1)]
    sent, tele, inverse, meta = start_values(teleport, sums, block)
    for step in range(HOPS):
        first, last = step == 0, step == HOPS - 1
        shards = spread(sent, "hst")
        if first:
            for j in range(2, split, 2):
                far[j][1], *shards[1:-1] = lax.optimization_barrier((far[j][1], *shards[1:-1]))
                far[j + 1].append(xor_send(far[j][1], "doc", 1))
            sets = [[tiles], [near]] + [far[j] for j in range(2, split)]
        outs = hop(first, last, meta, here, shards, sets, tele, inverse)
        sent = outs[0]
        if first:
            tele = outs[1]
    chunks = [outs[0]] + [xor_send(outs[j], "doc", j) for j in range(1, split)]
    return finish(here, chunks).T


def solution(mesh):
    placed = (
        P(("hst", "doc"), None),
        P(),
        P(),
        P(("hst", "doc")),
        P(("hst", "doc"), None, None),
        P(("hst", "doc")),
        P(("hst", "doc")),
        P(("hst", "doc")),
        P("hst"),
    )
    return jax.shard_map(
        body, mesh=mesh, in_specs=placed, out_specs=P(("hst", "doc"), None), check_vma=False
    )
```

profile of v0, /device:TPU:0, one launch (start us, length us, event | category | flops | bytes accessed | tf_op | source)
XLA Modules:
  0.0 126.8 jit_solution(4205800826074524512)
XLA Ops:
  0.0 0.5 collective-permute-start
  0.5 2.8 %slice.7 = bf16[48,128,128]{2,1,0:T(8,128)(2,1)} slice(bf16[64,128,128]{2,1,0:T(8,128)(2,1)} %rest_8_.5), slice={[0:48], [0:128], [0:128]} | slice | bytes 3145728 | tf_op jit(solution)/shard_map/slice | solution.py:420
  3.3 2.6 %collective-permute-start.4 = (bf16[48,128,128]{2,1,0:T(8,128)(2,1)}, bf16[48,128,128]{2,1,0:T(8,128)(2,1)}, u32[]{:S(2)}, u32[]{:S(2)}) collective-permute-start(bf16[48,128,128]{2,1,0:T(8,128)(2,1)} %slice.7), channel_id=1, source_target_pairs={{0,2},{1,3},{2,0},{3,1},{4,6},{5,7},{6,4},{7,5},{8,10},{9,11},{10,... | collective-permute-start | bytes 4718600 | tf_op jit(solution)/shard_map/ppermute | solution.py:24
  6.5 5.5 %column_sums.1 = f32[8,16,128]{2,1,0:T(8,128)} custom-call(s32[64]{0:T(128)} %source.1, s32[1]{0:T(128)} %copy.10.count, bf16[64,128,128]{2,1,0:T(8,128)(2,1)} %rest_8_.5), custom_call_target="tpu_custom_call" | custom-call | flops 1048576 | bytes 2097152 | tf_op jit(solution)/shard_map/column_sums/pallas_call | solution.py:50
  12.0 5.8 %all-to-all-start = ((f32[8,16,128]{2,1,0:T(8,128)}), f32[8,16,128]{2,1,0:T(8,128)S(1)}, u32[]{:S(2)}, u32[]{:S(2)}) async-start(f32[8,16,128]{2,1,0:T(8,128)} %column_sums.1), calls=%async_computation | async-start | bytes 131072 | tf_op jit(solution)/shard_map/all_to_all | solution.py:173
  17.9 8.2 %early_documents.1.carried = f32[512,512]{1,0:T(8,128)S(1)} custom-call(bf16[8192,768]{1,0:T(8,128)(2,1)} %docs.3, bf16[768,256]{1,0:T(8,128)(2,1)S(1)} %copy-done.13, bf16[64,256]{1,0:T(8,128)(2,1)S(1)} %bitcast.12, s32[8,1,1024]{2,1,0:T(1,128)S(1)} %bitcast.14), custom_call_target="tpu_custom_call" | custom-call | flops 3892314112 | bytes 6291456 | tf_op jit(solution)/shard_map/early_documents/pallas_call | solution.py:163
  26.1 1.0 copy-done.17
  27.1 1.3 %copy-done.1 = bf16[64,128,128]{2,1,0:T(8,128)(2,1)} copy-done((bf16[64,128,128]{2,1,0:T(8,128)(2,1)}, bf16[64,128,128]{2,1,0:T(8,128)(2,1)S(1)}, u32[]{:S(2)}) %copy-start.1) | copy-done | bytes 2097176
  28.4 1.2 copy-done.18
  29.7 8.5 %late_documents.1 = (f32[16,2304]{1,0:T(8,128)S(1)}, f32[16,2304]{1,0:T(8,128)S(1)}, f32[16,2304]{1,0:T(8,128)S(1)}, f32[16,2304]{1,0:T(8,128)S(1)}) custom-call(s32[1]{0:T(128)} %bitcast.1.place, bf16[8192,768]{1,0:T(8,128)(2,1)} %docs.3, bf16[768,256]{1,0:T(8,128)(2,1)S(1)} %copy-done.13, bf16[64,256]{1,0:T(8,128)(2,1)S(1)} %bitcast.13, ...), custom_call_target="tpu_custom_call" | custom-call | flops 3892314112 | bytes 6291456 | tf_op jit(solution)/shard_map/late_documents/pallas_call | solution.py:176
  38.3 0.6 collective-permute-start.2
  38.9 1.3 %collective-permute-start.3 = (f32[16,2304]{1,0:T(8,128)S(1)}, f32[16,2304]{1,0:T(8,128)S(1)}, u32[]{:S(2)}, u32[]{:S(2)}) collective-permute-start(f32[16,2304]{1,0:T(8,128)S(1)} %get-tuple-element.38), channel_id=1, source_target_pairs={{0,3},{1,2},{2,1},{3,0},{4,7},{5,6},{6,5},{7,4},{8,11},{9,10},{10,... | collective-permute-start | bytes 442376 | tf_op jit(solution)/shard_map/ppermute | solution.py:24
  40.2 1.0 collective-permute-done.4.rest_10_
  41.2 3.8 %collective-permute-done.2.rest_2_ = f32[16,2304]{1,0:T(8,128)S(1)} collective-permute-done((f32[16,2304]{1,0:T(8,128)S(1)}, f32[16,2304]{1,0:T(8,128)S(1)}, u32[]{:S(2)}, u32[]{:S(2)}) %collective-permute-start.2) | collective-permute-done | bytes 147488 | tf_op jit(solution)/shard_map/ppermute | solution.py:24
  45.0 2.3 %collective-permute-done.3.rest_3_ = f32[16,2304]{1,0:T(8,128)S(1)} collective-permute-done((f32[16,2304]{1,0:T(8,128)S(1)}, f32[16,2304]{1,0:T(8,128)S(1)}, u32[]{:S(2)}, u32[]{:S(2)}) %collective-permute-start.3) | collective-permute-done | bytes 147488 | tf_op jit(solution)/shard_map/ppermute | solution.py:24
  47.2 0.3 collective-permute-start.13
  47.5 1.4 %collective-permute-start.5 = (bf16[16,128,128]{2,1,0:T(8,128)(2,1)S(1)}, bf16[16,128,128]{2,1,0:T(8,128)(2,1)S(1)}, u32[]{:S(2)}, u32[]{:S(2)}) collective-permute-start(bf16[16,128,128]{2,1,0:T(8,128)(2,1)S(1)} %slice.6), channel_id=1, source_target_pairs={{0,2},{1,3},{2,0},{3,1},{4,6},{5,7},{6,4},{7,5},{8,10},{9,11},{10,... | collective-permute-start | bytes 1572872 | tf_op jit(solution)/shard_map/ppermute | solution.py:24
  49.1 3.7 %collective-permute-start.11 = (bf16[16,2176]{1,0:T(8,128)(2,1)S(1)}, bf16[16,2176]{1,0:T(8,128)(2,1)S(1)}, u32[]{:S(2)}, u32[]{:S(2)}) collective-permute-start(bf16[16,2176]{1,0:T(8,128)(2,1)S(1)} %get-tuple-element.44.rest_0_), channel_id=1, source_target_pairs={{0,24},{4,28},{8,16},{12,20},{16,8},{20,12},{24,0},{28,4},{1,25},{... | collective-permute-start | bytes 208904 | tf_op jit(solution)/shard_map/ppermute | solution.py:24
  52.8 0.8 collective-permute-start.7
  53.6 2.2 %collective-permute-done.11.rest_6_ = bf16[16,2176]{1,0:T(8,128)(2,1)S(1)} collective-permute-done((bf16[16,2176]{1,0:T(8,128)(2,1)S(1)}, bf16[16,2176]{1,0:T(8,128)(2,1)S(1)}, u32[]{:S(2)}, u32[]{:S(2)}) %collective-permute-start.11) | collective-permute-done | bytes 69664 | tf_op jit(solution)/shard_map/ppermute | solution.py:24
  55.8 1.5 %collective-permute-start.6 = (bf16[16,2176]{1,0:T(8,128)(2,1)S(1)}, bf16[16,2176]{1,0:T(8,128)(2,1)S(1)}, u32[]{:S(2)}, u32[]{:S(2)}) collective-permute-start(bf16[16,2176]{1,0:T(8,128)(2,1)S(1)} %get-tuple-element.44.rest_0_), channel_id=1, source_target_pairs={{0,4},{4,0},{8,12},{12,8},{16,20},{20,16},{24,28},{28,24},{1,5},{5... | collective-permute-start | bytes 208904 | tf_op jit(solution)/shard_map/ppermute | solution.py:24
  57.3 1.5 %collective-permute-done.9.rest_4_ = bf16[16,2176]{1,0:T(8,128)(2,1)S(1)} collective-permute-done((bf16[16,2176]{1,0:T(8,128)(2,1)S(1)}, bf16[16,2176]{1,0:T(8,128)(2,1)S(1)}, u32[]{:S(2)}, u32[]{:S(2)}) %collective-permute-start.9) | collective-permute-done | bytes 69664 | tf_op jit(solution)/shard_map/ppermute | solution.py:24
  58.8 1.5 %collective-permute-start.10 = (bf16[16,2176]{1,0:T(8,128)(2,1)S(1)}, bf16[16,2176]{1,0:T(8,128)(2,1)S(1)}, u32[]{:S(2)}, u32[]{:S(2)}) collective-permute-start(bf16[16,2176]{1,0:T(8,128)(2,1)S(1)} %collective-permute-done.9.rest_4_), channel_id=1, source_target_pairs={{0,4},{4,0},{8,12},{12,8},{16,20},{20,16},{24,28},{28,24},{1,5},{5... | collective-permute-start | bytes 208904 | tf_op jit(solution)/shard_map/ppermute | solution.py:24
  60.3 0.5 collective-permute-start.8
  60.8 0.6 copy-done.3
  61.4 0.6 copy-done.5
  62.1 1.6 %collective-permute-done.10.rest_5_ = bf16[16,2176]{1,0:T(8,128)(2,1)S(1)} collective-permute-done((bf16[16,2176]{1,0:T(8,128)(2,1)S(1)}, bf16[16,2176]{1,0:T(8,128)(2,1)S(1)}, u32[]{:S(2)}, u32[]{:S(2)}) %collective-permute-start.10) | collective-permute-done | bytes 69664 | tf_op jit(solution)/shard_map/ppermute | solution.py:24
  63.7 0.6 copy-done.7
  64.4 0.3 collective-permute-done.8.rest_3_
  64.6 0.6 copy-done.9
  65.3 0.8 collective-permute-start.12
  66.2 3.7 %collective-permute-done.12.rest_7_ = bf16[16,2176]{1,0:T(8,128)(2,1)S(1)} collective-permute-done((bf16[16,2176]{1,0:T(8,128)(2,1)S(1)}, bf16[16,2176]{1,0:T(8,128)(2,1)S(1)}, u32[]{:S(2)}, u32[]{:S(2)}) %collective-permute-start.12) | collective-permute-done | bytes 69664 | tf_op jit(solution)/shard_map/ppermute | solution.py:24
  69.9 1.6 %copy-done.2 = bf16[64,128,128]{2,1,0:T(8,128)(2,1)S(1)} copy-done((bf16[64,128,128]{2,1,0:T(8,128)(2,1)S(1)}, bf16[64,128,128]{2,1,0:T(8,128)(2,1)}, u32[]{:S(2)}) %copy-start.2) | copy-done | bytes 2097176
  71.5 0.9 copy-done.4
  72.4 0.9 copy-done.6
  73.2 0.9 copy-done.8
  74.1 0.9 copy-done.10
  75.0 6.4 %hop.3 = (bf16[16,2048]{1,0:T(8,128)(2,1)S(1)}, f32[16,2048]{1,0:T(8,128)S(1)}) custom-call(s32[12,128]{1,0:T(8,128)S(1)} %get-tuple-element.43.meta, s32[2]{0:T(128)S(1)} %pad_add_fusion.here, bf16[16,2176]{1,0:T(8,128)(2,1)S(1)} %get-tuple-element.44.rest_0_, bf16[16,2176]{1,0:T(8,128)(2,1)S(1)} %copy-done.6, bf16[16,2176]{1,0:T(8,128)(2,1)S(1)} %copy-done.4, ...), custom_call_target="tpu_custom_call" | custom-call | flops 134217728 | bytes 8388608 | tf_op jit(solution)/shard_map/hop/pallas_call | solution.py:355
  81.4 2.1 %collective-permute-start.20 = (bf16[16,2048]{1,0:T(8,128)(2,1)S(1)}, bf16[16,2048]{1,0:T(8,128)(2,1)S(1)}, u32[]{:S(2)}, u32[]{:S(2)}) collective-permute-start(bf16[16,2048]{1,0:T(8,128)(2,1)S(1)} %get-tuple-element.57.rest_0_), channel_id=1, source_target_pairs={{0,24},{4,28},{8,16},{12,20},{16,8},{20,12},{24,0},{28,4},{1,25},{... | collective-permute-start | bytes 196616 | tf_op jit(solution)/shard_map/ppermute | solution.py:24
  83.6 2.3 %collective-permute-start.16 = (bf16[16,2048]{1,0:T(8,128)(2,1)S(1)}, bf16[16,2048]{1,0:T(8,128)(2,1)S(1)}, u32[]{:S(2)}, u32[]{:S(2)}) collective-permute-start(bf16[16,2048]{1,0:T(8,128)(2,1)S(1)} %get-tuple-element.57.rest_0_), channel_id=1, source_target_pairs={{0,8},{4,12},{8,0},{12,4},{16,24},{20,28},{24,16},{28,20},{1,9},{5... | collective-permute-start | bytes 196616 | tf_op jit(solution)/shard_map/ppermute | solution.py:24
  86.1 1.7 %collective-permute-done.20.rest_6_ = bf16[16,2048]{1,0:T(8,128)(2,1)S(1)} collective-permute-done((bf16[16,2048]{1,0:T(8,128)(2,1)S(1)}, bf16[16,2048]{1,0:T(8,128)(2,1)S(1)}, u32[]{:S(2)}, u32[]{:S(2)}) %collective-permute-start.20) | collective-permute-done | bytes 65568 | tf_op jit(solution)/shard_map/ppermute | solution.py:24
  87.8 0.5 collective-permute-start.21
  88.4 1.4 %collective-permute-done.18.rest_4_ = bf16[16,2048]{1,0:T(8,128)(2,1)S(1)} collective-permute-done((bf16[16,2048]{1,0:T(8,128)(2,1)S(1)}, bf16[16,2048]{1,0:T(8,128)(2,1)S(1)}, u32[]{:S(2)}, u32[]{:S(2)}) %collective-permute-start.18) | collective-permute-done | bytes 65568 | tf_op jit(solution)/shard_map/ppermute | solution.py:24
  89.8 1.0 collective-permute-start.19
  90.8 1.0 collective-permute-start.17
  92.1 2.3 %collective-permute-done.19.rest_5_ = bf16[16,2048]{1,0:T(8,128)(2,1)S(1)} collective-permute-done((bf16[16,2048]{1,0:T(8,128)(2,1)S(1)}, bf16[16,2048]{1,0:T(8,128)(2,1)S(1)}, u32[]{:S(2)}, u32[]{:S(2)}) %collective-permute-start.19) | collective-permute-done | bytes 65568 | tf_op jit(solution)/shard_map/ppermute | solution.py:24
  94.4 0.7 collective-permute-done.17.rest_3_
  95.1 6.3 %hop.4.rest_0_ = bf16[16,2048]{1,0:T(8,128)(2,1)S(1)} custom-call(s32[12,128]{1,0:T(8,128)S(1)} %get-tuple-element.43.meta, s32[2]{0:T(128)S(1)} %pad_add_fusion.here, bf16[16,2048]{1,0:T(8,128)(2,1)S(1)} %get-tuple-element.57.rest_0_, bf16[16,2048]{1,0:T(8,128)(2,1)S(1)} %collective-permute-done.15.rest_1_, ...), custom_call_target="tpu_custom_call" | custom-call | flops 134217728 | bytes 8388608 | tf_op jit(solution)/shard_map/hop/pallas_call | solution.py:355
  101.4 2.0 %collective-permute-start.27 = (bf16[16,2048]{1,0:T(8,128)(2,1)S(1)}, bf16[16,2048]{1,0:T(8,128)(2,1)S(1)}, u32[]{:S(2)}, u32[]{:S(2)}) collective-permute-start(bf16[16,2048]{1,0:T(8,128)(2,1)S(1)} %hop.4.rest_0_), channel_id=1, source_target_pairs={{0,24},{4,28},{8,16},{12,20},{16,8},{20,12},{24,0},{28,4},{1,25},{... | collective-permute-start | bytes 196616 | tf_op jit(solution)/shard_map/ppermute | solution.py:24
  103.5 2.4 %collective-permute-start.23 = (bf16[16,2048]{1,0:T(8,128)(2,1)S(1)}, bf16[16,2048]{1,0:T(8,128)(2,1)S(1)}, u32[]{:S(2)}, u32[]{:S(2)}) collective-permute-start(bf16[16,2048]{1,0:T(8,128)(2,1)S(1)} %hop.4.rest_0_), channel_id=1, source_target_pairs={{0,8},{4,12},{8,0},{12,4},{16,24},{20,28},{24,16},{28,20},{1,9},{5... | collective-permute-start | bytes 196616 | tf_op jit(solution)/shard_map/ppermute | solution.py:24
  105.9 0.5 collective-permute-start.22
  106.4 1.8 %collective-permute-done.27.rest_6_ = bf16[16,2048]{1,0:T(8,128)(2,1)S(1)} collective-permute-done((bf16[16,2048]{1,0:T(8,128)(2,1)S(1)}, bf16[16,2048]{1,0:T(8,128)(2,1)S(1)}, u32[]{:S(2)}, u32[]{:S(2)}) %collective-permute-start.27) | collective-permute-done | bytes 65568 | tf_op jit(solution)/shard_map/ppermute | solution.py:24
  108.2 1.3 %collective-permute-done.25.rest_4_ = bf16[16,2048]{1,0:T(8,128)(2,1)S(1)} collective-permute-done((bf16[16,2048]{1,0:T(8,128)(2,1)S(1)}, bf16[16,2048]{1,0:T(8,128)(2,1)S(1)}, u32[]{:S(2)}, u32[]{:S(2)}) %collective-permute-start.25) | collective-permute-done | bytes 65568 | tf_op jit(solution)/shard_map/ppermute | solution.py:24
  109.5 0.9 collective-permute-start.26
  110.4 1.1 collective-permute-start.24
  111.5 1.5 %collective-permute-done.28.rest_7_ = bf16[16,2048]{1,0:T(8,128)(2,1)S(1)} collective-permute-done((bf16[16,2048]{1,0:T(8,128)(2,1)S(1)}, bf16[16,2048]{1,0:T(8,128)(2,1)S(1)}, u32[]{:S(2)}, u32[]{:S(2)}) %collective-permute-start.28) | collective-permute-done | bytes 65568 | tf_op jit(solution)/shard_map/ppermute | solution.py:24
  113.0 0.8 collective-permute-done.26.rest_5_
  113.9 0.8 collective-permute-done.24.rest_3_
  114.7 6.3 %hop.5 = (f32[16,512]{1,0:T(8,128)S(1)}, f32[16,512]{1,0:T(8,128)S(1)}, f32[16,512]{1,0:T(8,128)S(1)}, f32[16,512]{1,0:T(8,128)S(1)}) custom-call(s32[12,128]{1,0:T(8,128)S(1)} %get-tuple-element.43.meta, s32[2]{0:T(128)S(1)} %pad_add_fusion.here, bf16[16,2048]{1,0:T(8,128)(2,1)S(1)} %hop.4.rest_0_, bf16[16,2048]{1,0:T(8,128)(2,1)S(1)} %collective-permute-done.22.rest_1_, ...), custom_call_target="tpu_custom_call" | custom-call | flops 134217728 | bytes 8388608 | tf_op jit(solution)/shard_map/hop/pallas_call | solution.py:355
  121.1 1.2 collective-permute-start.30
  122.3 0.7 collective-permute-start.31
  123.0 2.1 %collective-permute-done.30.rest_2_ = f32[16,512]{1,0:T(8,128)S(1)} collective-permute-done((f32[16,512]{1,0:T(8,128)S(1)}, f32[16,512]{1,0:T(8,128)S(1)}, u32[]{:S(2)}, u32[]{:S(2)}) %collective-permute-start.30) | collective-permute-done | bytes 32800 | tf_op jit(solution)/shard_map/ppermute | solution.py:24
  125.1 0.6 collective-permute-done.31.rest_3_
  125.6 1.2 finish.1
  (51 shorter events, 1.0 us)
Async XLA Ops:
  0.0 17.8 %copy-start.13 = (bf16[768,256]{1,0:T(8,128)(2,1)S(1)}, bf16[768,256]{1,0:T(8,128)(2,1)}, u32[]{:S(2)}) copy-start(bf16[768,256]{1,0:T(8,128)(2,1)} %w_in.3) | copy-start | bytes 1179652
  0.0 17.9 %copy-start.15 = (s32[8192]{0:T(1024)S(1)}, s32[8192]{0:T(1024)}, u32[]{:S(2)}) copy-start(s32[8192]{0:T(1024)} %param.12) | copy-start | bytes 98308
  0.0 17.9 %copy-start.14 = (bf16[256,64]{0,1:T(8,128)(2,1)S(1)}, bf16[256,64]{0,1:T(8,128)(2,1)}, u32[]{:S(2)}) copy-start(bf16[256,64]{0,1:T(8,128)(2,1)} %param.11) | copy-start | bytes 98308
  0.0 27.1 %collective-permute-start = (bf16[64,128,128]{2,1,0:T(8,128)(2,1)}, bf16[64,128,128]{2,1,0:T(8,128)(2,1)S(1)}, u32[]{:S(2)}, u32[]{:S(2)}) collective-permute-start(bf16[64,128,128]{2,1,0:T(8,128)(2,1)} %rest_8_.5), channel_id=1, source_target_pairs={{0,1},{1,0},{2,3},{3,2},{4,5},{5,4},{6,7},{7,6},{8,9},{9,8},{10,11... | collective-permute-start | bytes 6291464 | tf_op jit(solution)/shard_map/ppermute | solution.py:24
  3.3 37.9 %collective-permute-start.4 = (bf16[48,128,128]{2,1,0:T(8,128)(2,1)}, bf16[48,128,128]{2,1,0:T(8,128)(2,1)}, u32[]{:S(2)}, u32[]{:S(2)}) collective-permute-start(bf16[48,128,128]{2,1,0:T(8,128)(2,1)} %slice.7), channel_id=1, source_target_pairs={{0,2},{1,3},{2,0},{3,1},{4,6},{5,7},{6,4},{7,5},{8,10},{9,11},{10,... | collective-permute-start | bytes 4718600 | tf_op jit(solution)/shard_map/ppermute | solution.py:24
  12.0 15.0 %all-to-all-start = ((f32[8,16,128]{2,1,0:T(8,128)}), f32[8,16,128]{2,1,0:T(8,128)S(1)}, u32[]{:S(2)}, u32[]{:S(2)}) async-start(f32[8,16,128]{2,1,0:T(8,128)} %column_sums.1), calls=%async_computation | async-start | bytes 131072 | tf_op jit(solution)/shard_map/all_to_all | solution.py:173
  17.9 10.6 %copy-start.12 = (s32[64]{0:T(128)S(1)}, s32[64]{0:T(128)}, u32[]{:S(2)}) copy-start(s32[64]{0:T(128)} %source.1) | copy-start | bytes 772
  17.9 10.5 %copy-start.16 = (s32[64]{0:T(128)S(1)}, s32[64]{0:T(128)}, u32[]{:S(2)}) copy-start(s32[64]{0:T(128)} %param.14) | copy-start | bytes 772
  26.1 1.0 copy-start.17
  27.1 1.4 %copy-start.1 = (bf16[64,128,128]{2,1,0:T(8,128)(2,1)}, bf16[64,128,128]{2,1,0:T(8,128)(2,1)S(1)}, u32[]{:S(2)}) copy-start(bf16[64,128,128]{2,1,0:T(8,128)(2,1)S(1)} %collective-permute-done.rest_9_) | copy-start | bytes 6291460
  28.4 1.2 copy-start.18
  29.7 10.5 %copy-start = (bf16[64,128,128]{2,1,0:T(8,128)(2,1)S(1)}, bf16[64,128,128]{2,1,0:T(8,128)(2,1)}, u32[]{:S(2)}) copy-start(bf16[64,128,128]{2,1,0:T(8,128)(2,1)} %rest_8_.5) | copy-start | bytes 6291460
  29.7 19.3 %copy-start.11 = (s32[2048]{0:T(1024)S(1)}, s32[2048]{0:T(1024)}, u32[]{:S(2)}) copy-start(s32[2048]{0:T(1024)} %param.17) | copy-start | bytes 24580
  38.2 3.0 %collective-permute-start.1 = (f32[16,2304]{1,0:T(8,128)S(1)}, f32[16,2304]{1,0:T(8,128)S(1)}, u32[]{:S(2)}, u32[]{:S(2)}) collective-permute-start(f32[16,2304]{1,0:T(8,128)S(1)} %get-tuple-element.36), channel_id=1, source_target_pairs={{0,1},{1,0},{2,3},{3,2},{4,5},{5,4},{6,7},{7,6},{8,9},{9,8},{10,11... | collective-permute-start | bytes 442376 | tf_op jit(solution)/shard_map/ppermute | solution.py:24
  38.3 6.7 %collective-permute-start.2 = (f32[16,2304]{1,0:T(8,128)S(1)}, f32[16,2304]{1,0:T(8,128)S(1)}, u32[]{:S(2)}, u32[]{:S(2)}) collective-permute-start(f32[16,2304]{1,0:T(8,128)S(1)} %get-tuple-element.37), channel_id=1, source_target_pairs={{0,2},{1,3},{2,0},{3,1},{4,6},{5,7},{6,4},{7,5},{8,10},{9,11},{10,... | collective-permute-start | bytes 442376 | tf_op jit(solution)/shard_map/ppermute | solution.py:24
  38.9 8.4 %collective-permute-start.3 = (f32[16,2304]{1,0:T(8,128)S(1)}, f32[16,2304]{1,0:T(8,128)S(1)}, u32[]{:S(2)}, u32[]{:S(2)}) collective-permute-start(f32[16,2304]{1,0:T(8,128)S(1)} %get-tuple-element.38), channel_id=1, source_target_pairs={{0,3},{1,2},{2,1},{3,0},{4,7},{5,6},{6,5},{7,4},{8,11},{9,10},{10,... | collective-permute-start | bytes 442376 | tf_op jit(solution)/shard_map/ppermute | solution.py:24
  47.2 22.6 %collective-permute-start.13 = (bf16[48,128,128]{2,1,0:T(8,128)(2,1)}, bf16[48,128,128]{2,1,0:T(8,128)(2,1)}, u32[]{:S(2)}, u32[]{:S(2)}) collective-permute-start(bf16[48,128,128]{2,1,0:T(8,128)(2,1)} %collective-permute-done.4.rest_10_), channel_id=1, source_target_pairs={{0,1},{1,0},{2,3},{3,2},{4,5},{5,4},{6,7},{7,6},{8,9},{9,8},{10,11... | collective-permute-start | bytes 4718600 | tf_op jit(solution)/shard_map/ppermute | solution.py:24
  47.5 17.8 %collective-permute-start.5 = (bf16[16,128,128]{2,1,0:T(8,128)(2,1)S(1)}, bf16[16,128,128]{2,1,0:T(8,128)(2,1)S(1)}, u32[]{:S(2)}, u32[]{:S(2)}) collective-permute-start(bf16[16,128,128]{2,1,0:T(8,128)(2,1)S(1)} %slice.6), channel_id=1, source_target_pairs={{0,2},{1,3},{2,0},{3,1},{4,6},{5,7},{6,4},{7,5},{8,10},{9,11},{10,... | collective-permute-start | bytes 1572872 | tf_op jit(solution)/shard_map/ppermute | solution.py:24
  49.1 6.7 %collective-permute-start.11 = (bf16[16,2176]{1,0:T(8,128)(2,1)S(1)}, bf16[16,2176]{1,0:T(8,128)(2,1)S(1)}, u32[]{:S(2)}, u32[]{:S(2)}) collective-permute-start(bf16[16,2176]{1,0:T(8,128)(2,1)S(1)} %get-tuple-element.44.rest_0_), channel_id=1, source_target_pairs={{0,24},{4,28},{8,16},{12,20},{16,8},{20,12},{24,0},{28,4},{1,25},{... | collective-permute-start | bytes 208904 | tf_op jit(solution)/shard_map/ppermute | solution.py:24
  52.8 6.0 %collective-permute-start.9 = (bf16[16,2176]{1,0:T(8,128)(2,1)S(1)}, bf16[16,2176]{1,0:T(8,128)(2,1)S(1)}, u32[]{:S(2)}, u32[]{:S(2)}) collective-permute-start(bf16[16,2176]{1,0:T(8,128)(2,1)S(1)} %get-tuple-element.44.rest_0_), channel_id=1, source_target_pairs={{0,16},{4,20},{8,24},{12,28},{16,0},{20,4},{24,8},{28,12},{1,17},{... | collective-permute-start | bytes 208904 | tf_op jit(solution)/shard_map/ppermute | solution.py:24
  52.8 7.6 %collective-permute-start.7 = (bf16[16,2176]{1,0:T(8,128)(2,1)S(1)}, bf16[16,2176]{1,0:T(8,128)(2,1)S(1)}, u32[]{:S(2)}, u32[]{:S(2)}) collective-permute-start(bf16[16,2176]{1,0:T(8,128)(2,1)S(1)} %get-tuple-element.44.rest_0_), channel_id=1, source_target_pairs={{0,8},{4,12},{8,0},{12,4},{16,24},{20,28},{24,16},{28,20},{1,9},{5... | collective-permute-start | bytes 208904 | tf_op jit(solution)/shard_map/ppermute | solution.py:24
  55.8 5.7 %collective-permute-start.6 = (bf16[16,2176]{1,0:T(8,128)(2,1)S(1)}, bf16[16,2176]{1,0:T(8,128)(2,1)S(1)}, u32[]{:S(2)}, u32[]{:S(2)}) collective-permute-start(bf16[16,2176]{1,0:T(8,128)(2,1)S(1)} %get-tuple-element.44.rest_0_), channel_id=1, source_target_pairs={{0,4},{4,0},{8,12},{12,8},{16,20},{20,16},{24,28},{28,24},{1,5},{5... | collective-permute-start | bytes 208904 | tf_op jit(solution)/shard_map/ppermute | solution.py:24
  58.8 4.9 %collective-permute-start.10 = (bf16[16,2176]{1,0:T(8,128)(2,1)S(1)}, bf16[16,2176]{1,0:T(8,128)(2,1)S(1)}, u32[]{:S(2)}, u32[]{:S(2)}) collective-permute-start(bf16[16,2176]{1,0:T(8,128)(2,1)S(1)} %collective-permute-done.9.rest_4_), channel_id=1, source_target_pairs={{0,4},{4,0},{8,12},{12,8},{16,20},{20,16},{24,28},{28,24},{1,5},{5... | collective-permute-start | bytes 208904 | tf_op jit(solution)/shard_map/ppermute | solution.py:24
  60.3 4.3 %collective-permute-start.8 = (bf16[16,2176]{1,0:T(8,128)(2,1)S(1)}, bf16[16,2176]{1,0:T(8,128)(2,1)S(1)}, u32[]{:S(2)}, u32[]{:S(2)}) collective-permute-start(bf16[16,2176]{1,0:T(8,128)(2,1)S(1)} %collective-permute-done.7.rest_2_), channel_id=1, source_target_pairs={{0,4},{4,0},{8,12},{12,8},{16,20},{20,16},{24,28},{28,24},{1,5},{5... | collective-permute-start | bytes 208904 | tf_op jit(solution)/shard_map/ppermute | solution.py:24
  60.8 0.6 copy-start.3
  61.4 0.6 copy-start.5
  63.7 0.6 copy-start.7
  64.6 0.6 copy-start.9
  65.3 4.6 %collective-permute-start.14 = (bf16[16,128,128]{2,1,0:T(8,128)(2,1)S(1)}, bf16[16,128,128]{2,1,0:T(8,128)(2,1)S(1)}, u32[]{:S(2)}, u32[]{:S(2)}) collective-permute-start(bf16[16,128,128]{2,1,0:T(8,128)(2,1)S(1)} %collective-permute-done.5.rest_11_), channel_id=1, source_target_pairs={{0,1},{1,0},{2,3},{3,2},{4,5},{5,4},{6,7},{7,6},{8,9},{9,8},{10,11... | collective-permute-start | bytes 1572872 | tf_op jit(solution)/shard_map/ppermute | solution.py:24
  65.3 4.6 %collective-permute-start.12 = (bf16[16,2176]{1,0:T(8,128)(2,1)S(1)}, bf16[16,2176]{1,0:T(8,128)(2,1)S(1)}, u32[]{:S(2)}, u32[]{:S(2)}) collective-permute-start(bf16[16,2176]{1,0:T(8,128)(2,1)S(1)} %collective-permute-done.11.rest_6_), channel_id=1, source_target_pairs={{0,4},{4,0},{8,12},{12,8},{16,20},{20,16},{24,28},{28,24},{1,5},{5... | collective-permute-start | bytes 208904 | tf_op jit(solution)/shard_map/ppermute | solution.py:24
  69.9 1.6 %copy-start.2 = (bf16[64,128,128]{2,1,0:T(8,128)(2,1)S(1)}, bf16[64,128,128]{2,1,0:T(8,128)(2,1)}, u32[]{:S(2)}) copy-start(bf16[64,128,128]{2,1,0:T(8,128)(2,1)} %copy-done.1) | copy-start | bytes 6291460
  71.5 0.9 copy-start.4
  72.4 0.9 copy-start.6
  73.2 0.9 copy-start.8
  74.1 0.9 copy-start.10
  81.4 6.4 %collective-permute-start.20 = (bf16[16,2048]{1,0:T(8,128)(2,1)S(1)}, bf16[16,2048]{1,0:T(8,128)(2,1)S(1)}, u32[]{:S(2)}, u32[]{:S(2)}) collective-permute-start(bf16[16,2048]{1,0:T(8,128)(2,1)S(1)} %get-tuple-element.57.rest_0_), channel_id=1, source_target_pairs={{0,24},{4,28},{8,16},{12,20},{16,8},{20,12},{24,0},{28,4},{1,25},{... | collective-permute-start | bytes 196616 | tf_op jit(solution)/shard_map/ppermute | solution.py:24
  83.6 6.2 %collective-permute-start.18 = (bf16[16,2048]{1,0:T(8,128)(2,1)S(1)}, bf16[16,2048]{1,0:T(8,128)(2,1)S(1)}, u32[]{:S(2)}, u32[]{:S(2)}) collective-permute-start(bf16[16,2048]{1,0:T(8,128)(2,1)S(1)} %get-tuple-element.57.rest_0_), channel_id=1, source_target_pairs={{0,16},{4,20},{8,24},{12,28},{16,0},{20,4},{24,8},{28,12},{1,17},{... | collective-permute-start | bytes 196616 | tf_op jit(solution)/shard_map/ppermute | solution.py:24
  83.6 7.2 %collective-permute-start.16 = (bf16[16,2048]{1,0:T(8,128)(2,1)S(1)}, bf16[16,2048]{1,0:T(8,128)(2,1)S(1)}, u32[]{:S(2)}, u32[]{:S(2)}) collective-permute-start(bf16[16,2048]{1,0:T(8,128)(2,1)S(1)} %get-tuple-element.57.rest_0_), channel_id=1, source_target_pairs={{0,8},{4,12},{8,0},{12,4},{16,24},{20,28},{24,16},{28,20},{1,9},{5... | collective-permute-start | bytes 196616 | tf_op jit(solution)/shard_map/ppermute | solution.py:24
  85.9 6.0 %collective-permute-start.15 = (bf16[16,2048]{1,0:T(8,128)(2,1)S(1)}, bf16[16,2048]{1,0:T(8,128)(2,1)S(1)}, u32[]{:S(2)}, u32[]{:S(2)}) collective-permute-start(bf16[16,2048]{1,0:T(8,128)(2,1)S(1)} %get-tuple-element.57.rest_0_), channel_id=1, source_target_pairs={{0,4},{4,0},{8,12},{12,8},{16,20},{20,16},{24,28},{28,24},{1,5},{5... | collective-permute-start | bytes 196616 | tf_op jit(solution)/shard_map/ppermute | solution.py:24
  87.8 4.3 %collective-permute-start.21 = (bf16[16,2048]{1,0:T(8,128)(2,1)S(1)}, bf16[16,2048]{1,0:T(8,128)(2,1)S(1)}, u32[]{:S(2)}, u32[]{:S(2)}) collective-permute-start(bf16[16,2048]{1,0:T(8,128)(2,1)S(1)} %collective-permute-done.20.rest_6_), channel_id=1, source_target_pairs={{0,4},{4,0},{8,12},{12,8},{16,20},{20,16},{24,28},{28,24},{1,5},{5... | collective-permute-start | bytes 196616 | tf_op jit(solution)/shard_map/ppermute | solution.py:24
  89.8 4.6 %collective-permute-start.19 = (bf16[16,2048]{1,0:T(8,128)(2,1)S(1)}, bf16[16,2048]{1,0:T(8,128)(2,1)S(1)}, u32[]{:S(2)}, u32[]{:S(2)}) collective-permute-start(bf16[16,2048]{1,0:T(8,128)(2,1)S(1)} %collective-permute-done.18.rest_4_), channel_id=1, source_target_pairs={{0,4},{4,0},{8,12},{12,8},{16,20},{20,16},{24,28},{28,24},{1,5},{5... | collective-permute-start | bytes 196616 | tf_op jit(solution)/shard_map/ppermute | solution.py:24
  90.8 4.3 %collective-permute-start.17 = (bf16[16,2048]{1,0:T(8,128)(2,1)S(1)}, bf16[16,2048]{1,0:T(8,128)(2,1)S(1)}, u32[]{:S(2)}, u32[]{:S(2)}) collective-permute-start(bf16[16,2048]{1,0:T(8,128)(2,1)S(1)} %collective-permute-done.16.rest_2_), channel_id=1, source_target_pairs={{0,4},{4,0},{8,12},{12,8},{16,20},{20,16},{24,28},{28,24},{1,5},{5... | collective-permute-start | bytes 196616 | tf_op jit(solution)/shard_map/ppermute | solution.py:24
  101.4 6.7 %collective-permute-start.27 = (bf16[16,2048]{1,0:T(8,128)(2,1)S(1)}, bf16[16,2048]{1,0:T(8,128)(2,1)S(1)}, u32[]{:S(2)}, u32[]{:S(2)}) collective-permute-start(bf16[16,2048]{1,0:T(8,128)(2,1)S(1)} %hop.4.rest_0_), channel_id=1, source_target_pairs={{0,24},{4,28},{8,16},{12,20},{16,8},{20,12},{24,0},{28,4},{1,25},{... | collective-permute-start | bytes 196616 | tf_op jit(solution)/shard_map/ppermute | solution.py:24
  103.5 6.0 %collective-permute-start.25 = (bf16[16,2048]{1,0:T(8,128)(2,1)S(1)}, bf16[16,2048]{1,0:T(8,128)(2,1)S(1)}, u32[]{:S(2)}, u32[]{:S(2)}) collective-permute-start(bf16[16,2048]{1,0:T(8,128)(2,1)S(1)} %hop.4.rest_0_), channel_id=1, source_target_pairs={{0,16},{4,20},{8,24},{12,28},{16,0},{20,4},{24,8},{28,12},{1,17},{... | collective-permute-start | bytes 196616 | tf_op jit(solution)/shard_map/ppermute | solution.py:24
  103.5 6.9 %collective-permute-start.23 = (bf16[16,2048]{1,0:T(8,128)(2,1)S(1)}, bf16[16,2048]{1,0:T(8,128)(2,1)S(1)}, u32[]{:S(2)}, u32[]{:S(2)}) collective-permute-start(bf16[16,2048]{1,0:T(8,128)(2,1)S(1)} %hop.4.rest_0_), channel_id=1, source_target_pairs={{0,8},{4,12},{8,0},{12,4},{16,24},{20,28},{24,16},{28,20},{1,9},{5... | collective-permute-start | bytes 196616 | tf_op jit(solution)/shard_map/ppermute | solution.py:24
  105.9 5.6 %collective-permute-start.22 = (bf16[16,2048]{1,0:T(8,128)(2,1)S(1)}, bf16[16,2048]{1,0:T(8,128)(2,1)S(1)}, u32[]{:S(2)}, u32[]{:S(2)}) collective-permute-start(bf16[16,2048]{1,0:T(8,128)(2,1)S(1)} %hop.4.rest_0_), channel_id=1, source_target_pairs={{0,4},{4,0},{8,12},{12,8},{16,20},{20,16},{24,28},{28,24},{1,5},{5... | collective-permute-start | bytes 196616 | tf_op jit(solution)/shard_map/ppermute | solution.py:24
  108.2 4.9 %collective-permute-start.28 = (bf16[16,2048]{1,0:T(8,128)(2,1)S(1)}, bf16[16,2048]{1,0:T(8,128)(2,1)S(1)}, u32[]{:S(2)}, u32[]{:S(2)}) collective-permute-start(bf16[16,2048]{1,0:T(8,128)(2,1)S(1)} %collective-permute-done.27.rest_6_), channel_id=1, source_target_pairs={{0,4},{4,0},{8,12},{12,8},{16,20},{20,16},{24,28},{28,24},{1,5},{5... | collective-permute-start | bytes 196616 | tf_op jit(solution)/shard_map/ppermute | solution.py:24
  109.5 4.3 %collective-permute-start.26 = (bf16[16,2048]{1,0:T(8,128)(2,1)S(1)}, bf16[16,2048]{1,0:T(8,128)(2,1)S(1)}, u32[]{:S(2)}, u32[]{:S(2)}) collective-permute-start(bf16[16,2048]{1,0:T(8,128)(2,1)S(1)} %collective-permute-done.25.rest_4_), channel_id=1, source_target_pairs={{0,4},{4,0},{8,12},{12,8},{16,20},{20,16},{24,28},{28,24},{1,5},{5... | collective-permute-start | bytes 196616 | tf_op jit(solution)/shard_map/ppermute | solution.py:24
  110.4 4.3 %collective-permute-start.24 = (bf16[16,2048]{1,0:T(8,128)(2,1)S(1)}, bf16[16,2048]{1,0:T(8,128)(2,1)S(1)}, u32[]{:S(2)}, u32[]{:S(2)}) collective-permute-start(bf16[16,2048]{1,0:T(8,128)(2,1)S(1)} %collective-permute-done.23.rest_2_), channel_id=1, source_target_pairs={{0,4},{4,0},{8,12},{12,8},{16,20},{20,16},{24,28},{28,24},{1,5},{5... | collective-permute-start | bytes 196616 | tf_op jit(solution)/shard_map/ppermute | solution.py:24
  121.0 1.9 %collective-permute-start.29 = (f32[16,512]{1,0:T(8,128)S(1)}, f32[16,512]{1,0:T(8,128)S(1)}, u32[]{:S(2)}, u32[]{:S(2)}) collective-permute-start(f32[16,512]{1,0:T(8,128)S(1)} %get-tuple-element.60), channel_id=1, source_target_pairs={{0,1},{1,0},{2,3},{3,2},{4,5},{5,4},{6,7},{7,6},{8,9},{9,8},{10,11... | collective-permute-start | bytes 98312 | tf_op jit(solution)/shard_map/ppermute | solution.py:24
  121.1 4.0 %collective-permute-start.30 = (f32[16,512]{1,0:T(8,128)S(1)}, f32[16,512]{1,0:T(8,128)S(1)}, u32[]{:S(2)}, u32[]{:S(2)}) collective-permute-start(f32[16,512]{1,0:T(8,128)S(1)} %get-tuple-element.61), channel_id=1, source_target_pairs={{0,2},{1,3},{2,0},{3,1},{4,6},{5,7},{6,4},{7,5},{8,10},{9,11},{10,... | collective-permute-start | bytes 98312 | tf_op jit(solution)/shard_map/ppermute | solution.py:24
  122.3 3.3 %collective-permute-start.31 = (f32[16,512]{1,0:T(8,128)S(1)}, f32[16,512]{1,0:T(8,128)S(1)}, u32[]{:S(2)}, u32[]{:S(2)}) collective-permute-start(f32[16,512]{1,0:T(8,128)S(1)} %get-tuple-element.62), channel_id=1, source_target_pairs={{0,3},{1,2},{2,1},{3,0},{4,7},{5,6},{6,5},{7,4},{8,11},{9,10},{10,... | collective-permute-start | bytes 98312 | tf_op jit(solution)/shard_map/ppermute | solution.py:24
where the time goes:
time: 127 us
  Pallas kernels  42.6 us (34%)
  starting transfers between devices  37.5 us (30%)
  waiting for transfers between devices  31.8 us (25%)
  local copies, waits for them, and re-layouts  14 us (11%)
    ppermute x32, waiting for transfers between devices, xor_send(): return lax.ppermute(value, axis, [(i, i ^ step) for i in range(size)])  31.8 us
    ppermute x32, starting transfers between devices, xor_send(): return lax.ppermute(value, axis, [(i, i ^ step) for i in range(size)])  31.7 us
    pallas_call x3, Pallas kernels, hop(): pl.pallas_call(functools.partial(hop_kernel, first, last, parts, spans, f...  19 us
    unnamed x38, local copies, waits for them, and re-layouts  11.2 us
    pallas_call x1, Pallas kernels, documents(): pl.pallas_call(late_documents_kernel, grid_spec=pltpu.PrefetchScalarGridS...  8.53 us
    pallas_call x1, Pallas kernels, documents(): pl.pallas_call(early_documents_kernel, grid=(half,), in_specs=specs(0), o...  8.18 us
    all_to_all x1, starting transfers between devices, documents(): lax.all_to_all(degree_parts, 'hst', split_axis=0, concat_axis=0, tiled=True)  5.82 us
    pallas_call x1, Pallas kernels, column_sums(): pl.pallas_call(column_sum_kernel, grid_spec=pltpu.PrefetchScalarGridSpec(...  5.49 us
  transfers between devices with their start and end apart: 33, of which 20 were waited for; matrix products, arithmetic and copies ran while one was open for 2% of the time, Pallas kernels for 18%

commit v1 on v0

--- a/solution.py
+++ b/solution.py
@@ -24,7 +24,7 @@
     return lax.ppermute(value, axis, [(i, i ^ step) for i in range(size)])
 
 
-def column_sum_kernel(source, count, tiles, out, total):
+def column_sum_kernel(cut, source, count, tiles, out, early, late, total):
     step = pl.program_id(0)
     parts, rows, _ = out.shape
 
@@ -32,8 +32,16 @@
     def _():
         total[...] = jnp.zeros_like(total)
 
-    for i in range(GROUP):
-        k = step * GROUP + i
+    @pl.when(step < cut)
+    def _():
+        early[...] = tiles[...]
+
+    @pl.when(step >= cut)
+    def _():
+        late[...] = tiles[...]
+
+    for i in range(TILE_GROUP):
+        k = step * TILE_GROUP + i
         row = jnp.where(k < count[0], source[k], parts * rows)
         part = jnp.sum(tiles[i].astype(jnp.float32), axis=0, keepdims=True)
         total[pl.ds(row, 1), :] += part
@@ -47,19 +55,30 @@
 def column_sums(source, count, tiles, parts, rows):
     slots, block, _ = tiles.shape
     shape = (parts, rows, block)
+    steps = slots // TILE_GROUP
+    cut = steps * EARLY_TILES // 64
+    group = (TILE_GROUP, block, block)
     return pl.pallas_call(
-        column_sum_kernel,
+        functools.partial(column_sum_kernel, cut),
         grid_spec=pltpu.PrefetchScalarGridSpec(
             num_scalar_prefetch=2,
-            grid=(slots // GROUP,),
-            in_specs=[pl.BlockSpec((GROUP, block, block), lambda i, s, c: (i, 0, 0))],
-            out_specs=pl.BlockSpec(shape, lambda i, s, c: (0, 0, 0)),
+            grid=(steps,),
+            in_specs=[pl.BlockSpec(group, lambda i, s, c: (i, 0, 0))],
+            out_specs=[
+                pl.BlockSpec(shape, lambda i, s, c: (0, 0, 0)),
+                pl.BlockSpec(group, lambda i, s, c: (jnp.minimum(i, cut - 1), 0, 0)),
+                pl.BlockSpec(group, lambda i, s, c: (jnp.maximum(i - cut, 0), 0, 0)),
+            ],
             scratch_shapes=[pltpu.VMEM((parts * rows + 8, block), jnp.float32)],
         ),
-        out_shape=jax.ShapeDtypeStruct(shape, jnp.float32),
-        compiler_params=pltpu.CompilerParams(vmem_limit_bytes=56 * MIB),
+        out_shape=[
+            jax.ShapeDtypeStruct(shape, jnp.float32),
+            jax.ShapeDtypeStruct((cut * TILE_GROUP, block, block), tiles.dtype),
+            jax.ShapeDtypeStruct(((steps - cut) * TILE_GROUP, block, block), tiles.dtype),
+        ],
+        compiler_params=pltpu.CompilerParams(vmem_limit_bytes=16 * MIB),
         cost_estimate=pl.CostEstimate(
-            flops=tiles.size, bytes_accessed=tiles.size * 2, transcendentals=0
+            flops=tiles.size, bytes_accessed=tiles.size * 4, transcendentals=0
         ),
         name="column_sums",
     )(source, count, tiles)
@@ -84,20 +103,7 @@
     return lax.dot_general(left, right, NT, preferred_element_type=jnp.float32)
 
 
-def early_documents_kernel(docs, w_in, w_out_t, host, total):
-    step = pl.program_id(0)
-    added = block_topics(docs, w_in, w_out_t, host, total.shape[1])
-
-    @pl.when(step == 0)
-    def _():
-        total[...] = added
-
-    @pl.when(step > 0)
-    def _():
-        total[...] += added
-
-
-def late_documents_kernel(place, docs, w_in, w_out_t, host, carried, degrees, *rest):
+def documents_kernel(place, docs, w_in, w_out_t, host, *rest):
     labels, outs, total = rest[:LABELS], rest[LABELS:-1], rest[-1]
     step = pl.program_id(0)
     topics = w_out_t.shape[0]
@@ -106,7 +112,7 @@
 
     @pl.when(step == 0)
     def _():
-        total[...] = carried[...] + added
+        total[...] = added
 
     @pl.when(step > 0)
     def _():
@@ -116,104 +122,67 @@
     def _():
         per = outs[0].shape[0]
         hosts = DIGITS * width
-        degree = sum(degrees[j] for j in range(1, degrees.shape[0])) + degrees[0]
-        blocks, block = degree.shape
-        wide = hosts + blocks // per * block
         for j, out in enumerate(outs):
             chunk = (place[0] ^ j) * per
             for d in range(DIGITS):
                 first = pl.ds(pl.multiple_of(d * topics + chunk, 8), per)
                 second = pl.ds(pl.multiple_of((DIGITS + d) * topics + chunk, 8), per)
                 out[:, d * width : (d + 1) * width] = total[first, :] + total[second, :]
-            for c in range(blocks // per):
-                cols = slice(hosts + c * block, hosts + (c + 1) * block)
-                out[:, cols] = degree[c * per : (c + 1) * per, :]
-            out[:, wide:] = jnp.zeros((per, block), jnp.float32)
+            out[:, hosts:] = jnp.zeros((per, out.shape[1] - hosts), jnp.float32)
             for r, label in enumerate(labels):
-                out[r : r + 1, wide : wide + label.shape[1]] = label[...].astype(jnp.float32)
-
-
-def documents(docs, w_in, w_out, doc_host, hosts, split, place, degree_parts, labels, ready):
+                out[r : r + 1, hosts : hosts + label.shape[1]] = label[...].astype(jnp.float32)
+
+
+def documents(docs, w_in, w_out, doc_host, hosts, split, place, labels, block):
     count, depth = docs.shape
     hid, topics = w_out.shape
     per = topics // split
     width = hosts // DIGITS
     steps = count // DOC_BLOCK
-    half = steps // 2
-    host = doc_host.reshape(steps, 1, DOC_BLOCK)
-    w_out_t = w_out.T
-
-    def specs(start):
-        return [
-            pl.BlockSpec((DOC_BLOCK, depth), lambda i, *_: (i + start, 0)),
-            pl.BlockSpec((depth, hid), lambda i, *_: (0, 0)),
-            pl.BlockSpec((topics, hid), lambda i, *_: (0, 0)),
-            pl.BlockSpec((1, 1, DOC_BLOCK), lambda i, *_: (i + start, 0, 0)),
-        ]
-
-    def cost(blocks):
-        rows = blocks * DOC_BLOCK
-        return pl.CostEstimate(
-            flops=2 * rows * (depth * hid + hid * topics + 2 * topics * hosts),
-            bytes_accessed=rows * depth * 2,
-            transcendentals=rows * (hid + topics),
-        )
-
-    held = (2 * DIGITS * topics, width)
-    carried = pl.pallas_call(
-        early_documents_kernel,
-        grid=(half,),
-        in_specs=specs(0),
-        out_specs=pl.BlockSpec(held, lambda i: (0, 0)),
-        out_shape=jax.ShapeDtypeStruct(held, jnp.float32),
-        compiler_params=pltpu.CompilerParams(vmem_limit_bytes=50 * MIB),
-        cost_estimate=cost(half),
-        name="early_documents",
-    )(docs, w_in, w_out_t, host)
-    degrees = lax.all_to_all(degree_parts, "hst", split_axis=0, concat_axis=0, tiled=True)
-    degrees, ready = lax.optimization_barrier((degrees, ready))
-    shape = (per, hosts + hosts // per + degrees.shape[2])
-    sums = pl.pallas_call(
-        late_documents_kernel,
+    shape = (per, hosts + block)
+    return pl.pallas_call(
+        documents_kernel,
         grid_spec=pltpu.PrefetchScalarGridSpec(
             num_scalar_prefetch=1,
-            grid=(steps - half,),
-            in_specs=specs(half)
-            + [
-                pl.BlockSpec(held, lambda i, p: (0, 0)),
-                pl.BlockSpec(degrees.shape, lambda i, p: (0, 0, 0)),
+            grid=(steps,),
+            in_specs=[
+                pl.BlockSpec((DOC_BLOCK, depth), lambda i, p: (i, 0)),
+                pl.BlockSpec((depth, hid), lambda i, p: (0, 0)),
+                pl.BlockSpec((topics, hid), lambda i, p: (0, 0)),
+                pl.BlockSpec((1, 1, DOC_BLOCK), lambda i, p: (i, 0, 0)),
             ]
             + [pl.BlockSpec(label.shape, lambda i, p: (0, 0)) for label in labels],
             out_specs=[pl.BlockSpec(shape, lambda i, p: (0, 0))] * split,
-            scratch_shapes=[pltpu.VMEM(held, jnp.float32)],
+            scratch_shapes=[pltpu.VMEM((2 * DIGITS * topics, width), jnp.float32)],
         ),
         out_shape=[jax.ShapeDtypeStruct(shape, jnp.float32)] * split,
-        compiler_params=pltpu.CompilerParams(vmem_limit_bytes=50 * MIB),
-        cost_estimate=cost(steps - half),
-        name="late_documents",
-    )(place, docs, w_in, w_out_t, host, carried, degrees, *labels)
-    return sums, ready
+        compiler_params=pltpu.CompilerParams(vmem_limit_bytes=48 * MIB),
+        cost_estimate=pl.CostEstimate(
+            flops=2 * count * (depth * hid + hid * topics + 2 * topics * hosts),
+            bytes_accessed=docs.size * 2,
+            transcendentals=count * (hid + topics),
+        ),
+        name="documents",
+    )(place, docs, w_in, w_out.T, doc_host.reshape(steps, 1, DOC_BLOCK), *labels)
 
 
 def start_kernel(teleport, *rest):
-    sums, (sent, start, inverse, meta) = rest[:-4], rest[-4:]
+    (sent, start, inverse, meta), rest = rest[-4:], rest[:-4]
+    sums, degrees = rest[: len(rest) // 2], rest[len(rest) // 2 :]
     per, hosts = start.shape
     blocks, block = teleport.shape
     member = teleport[...].astype(jnp.float32) * LIFT
     mass = jnp.zeros((per, 1), jnp.float32)
-    tail = slice(hosts, hosts + inverse.shape[1])
-    inv = 1.0 / jnp.maximum(sum(s[:, tail] for s in sums[1:]) + sums[0][:, tail], 1.0)
+    inv = 1.0 / jnp.maximum(sum(d[...] for d in degrees[1:]) + degrees[0][...], 1.0)
     inverse[...] = inv
     for j, s in enumerate(sums):
-        meta[j * LABELS : (j + 1) * LABELS, :] = s[:LABELS, tail.stop :].astype(jnp.int32)
+        meta[j * LABELS : (j + 1) * LABELS, :] = s[:LABELS, hosts:].astype(jnp.int32)
     for b in range(blocks):
         cols = slice(b * block, (b + 1) * block)
         value = sum(s[:, cols] for s in sums[1:]) + sums[0][:, cols]
         value = value * member[b : b + 1, :]
         start[:, cols] = value
-        c, r = b // per, b % per
-        row = inv[r : r + 1, c * block : (c + 1) * block]
-        sent[:, cols] = (value * row).astype(jnp.bfloat16)
+        sent[:, cols] = (value * inv[b : b + 1, :]).astype(jnp.bfloat16)
         mass = mass + jnp.sum(value, axis=1, keepdims=True)
     lane = lax.broadcasted_iota(jnp.int32, (per, block), 1)
     first = mass.astype(jnp.bfloat16).astype(jnp.float32)
@@ -225,23 +194,24 @@
     sent[:, blocks * block :] = pieces.astype(jnp.bfloat16)
 
 
-def start_values(teleport, sums, block):
+def start_values(teleport, sums, degrees):
     per, _ = sums[0].shape
     hosts = teleport.shape[0]
+    block = degrees[0].shape[1]
     vmem = pl.BlockSpec(memory_space=pltpu.VMEM)
     return pl.pallas_call(
         start_kernel,
-        in_specs=[vmem] * (1 + len(sums)),
+        in_specs=[vmem] * (1 + 2 * len(sums)),
         out_specs=[vmem] * 4,
         out_shape=[
             jax.ShapeDtypeStruct((per, hosts + block), jnp.bfloat16),
             jax.ShapeDtypeStruct((per, hosts), jnp.float32),
-            jax.ShapeDtypeStruct((per, hosts // per), jnp.float32),
+            jax.ShapeDtypeStruct(degrees[0].shape, jnp.float32),
             jax.ShapeDtypeStruct((len(sums) * LABELS, block), jnp.int32),
         ],
         compiler_params=pltpu.CompilerParams(vmem_limit_bytes=16 * MIB),
         name="start_values",
-    )(teleport.reshape(hosts // block, block), *sums)
+    )(teleport.reshape(hosts // block, block), *sums, *degrees)
 
 
 def hop_kernel(first, last, parts, spans, scale, meta, here, *rest):
@@ -309,9 +279,7 @@
             if last:
                 inflow[b] = state * scale
             else:
-                c, r = b // per, b % per
-                row = inverse[r : r + 1, c * block : (c + 1) * block]
-                outs[0][:, cols] = (state * row).astype(jnp.bfloat16)
+                outs[0][:, cols] = (state * inverse[b : b + 1, :]).astype(jnp.bfloat16)
         if last:
             count = outs[0].shape[1] // block
             for j, out in enumerate(outs):
@@ -416,25 +384,25 @@
     labels = [label.reshape(1, -1) for label in (src_block, dst_block, tile_count)]
 
     near = xor_send(tiles, "doc", 1)
-    cut = slots * EARLY_TILES // 64
-    early, late = tiles[:cut], tiles[cut:]
+    degree_parts, early, late = column_sums(src_block, tile_count, tiles, parts, blocks)
     far = {j: [xor_send(early, "doc", j)] for j in range(2, split, 2)}
-    degree_parts = column_sums(src_block, tile_count, tiles, parts, blocks)
-    sums, near = documents(
-        docs, w_in, w_out, doc_host, hosts, split, place.reshape(1), degree_parts, labels, near
-    )
+    degree_parts = lax.all_to_all(degree_parts, "hst", split_axis=0, concat_axis=0, tiled=True)
+    sums = list(documents(docs, w_in, w_out, doc_host, hosts, split, place.reshape(1), labels, block))
+    degree_parts, sums[0] = lax.optimization_barrier((degree_parts, sums[0]))
+    degree = jnp.sum(degree_parts, axis=0)
+    degrees = [degree] + [xor_send(degree, "doc", j) for j in range(1, split)]
     sums = [sums[0]] + [xor_send(sums[j], "doc", j) for j in range(1, split)]
-    sums, late, far = lax.optimization_barrier((sums, late, far))
+    late, far, _ = lax.optimization_barrier((late, far, sums[1:]))
     for j in range(2, split, 2):
         far[j].append(xor_send(late, "doc", j))
         far[j + 1] = [xor_send(far[j][0], "doc", 1)]
-    sent, tele, inverse, meta = start_values(teleport, sums, block)
+    sent, tele, inverse, meta = start_values(teleport, sums, degrees)
     for step in range(HOPS):
         first, last = step == 0, step == HOPS - 1
         shards = spread(sent, "hst")
         if first:
             for j in range(2, split, 2):
-                far[j][1], *shards[1:-1] = lax.optimization_barrier((far[j][1], *shards[1:-1]))
+                far[j][1], _ = lax.optimization_barrier((far[j][1], shards[1:-1]))
                 far[j + 1].append(xor_send(far[j][1], "doc", 1))
             sets = [[tiles], [near]] + [far[j] for j in range(2, split)]
         outs = hop(first, last, meta, here, shards, sets, tele, inverse)

time: 127 us -> 147 us (1.16)
  waiting for transfers between devices: 31.8 us -> 51.7 us
  blocking collectives: 0 us -> 12.5 us
  local copies, waits for them, and re-layouts: 14 us -> 6.7 us
  Pallas kernels: 42.6 us -> 39.6 us
  starting transfers between devices: 37.5 us -> 35.9 us
    ppermute x32 -> x35, waiting for transfers between devices: 31.8 us -> 51.7 us  [xor_send(): return lax.ppermute(value, axis, [(i, i ^ step) for i in range(size)])]
    all_to_all x0 -> x1, blocking collectives: none -> 12.5 us  [body(): lax.all_to_all(degree_parts, 'hst', split_axis=0, concat_axis=0, tiled=True)]
    all_to_all x1 -> x0, starting transfers between devices: 5.82 us -> none  [documents(): lax.all_to_all(degree_parts, 'hst', split_axis=0, concat_axis=0, tiled=True)]
    unnamed x38 -> x30, local copies, waits for them, and re-layouts: 11.2 us -> 6.7 us
    ppermute x32 -> x35, starting transfers between devices: 31.7 us -> 35.9 us  [xor_send(): return lax.ppermute(value, axis, [(i, i ^ step) for i in range(size)])]
    slice x2 -> x0, local copies, waits for them, and re-layouts: 2.8 us -> none  [body(): early, late = (tiles[:cut], tiles[cut:])]
    pallas_call x4 -> x3, Pallas kernels: 22.3 us -> 20 us  [the longest x1 15.1 us: documents(): pl.pallas_call(documents_kernel, grid_spec=pltpu.PrefetchScalarGridSpec(n...]
  transfers between devices with their start and end apart: 33 -> 35, of which waited for: 20 -> 21; matrix products, arithmetic and copies ran while one was open for 2% -> 0% of each run, Pallas kernels for 18% -> 10%
where the time goes in v1:
time: 147 us
  waiting for transfers between devices  51.7 us (35%)
  Pallas kernels  39.6 us (27%)
  starting transfers between devices  35.9 us (24%)
  blocking collectives  12.5 us (9%)
  local copies, waits for them, and re-layouts  6.7 us (5%)
    ppermute x35, waiting for transfers between devices, xor_send(): return lax.ppermute(value, axis, [(i, i ^ step) for i in range(size)])  51.7 us
    ppermute x35, starting transfers between devices, xor_send(): return lax.ppermute(value, axis, [(i, i ^ step) for i in range(size)])  35.9 us
    pallas_call x3, Pallas kernels, hop(): pl.pallas_call(functools.partial(hop_kernel, first, last, parts, spans, f...  18.3 us
    pallas_call x1, Pallas kernels, documents(): pl.pallas_call(documents_kernel, grid_spec=pltpu.PrefetchScalarGridSpec(n...  15.1 us
    all_to_all x1, blocking collectives, body(): lax.all_to_all(degree_parts, 'hst', split_axis=0, concat_axis=0, tiled=True)  12.5 us
    unnamed x30, local copies, waits for them, and re-layouts  6.7 us
    pallas_call x1, Pallas kernels, column_sums(): pl.pallas_call(functools.partial(column_sum_kernel, cut), grid_spec=pltpu...  4.77 us
  transfers between devices with their start and end apart: 35, of which 21 were waited for; matrix products, arithmetic and copies ran while one was open for 0% of the time, Pallas kernels for 10%

profile of v1, /device:TPU:0, one launch (start us, length us, event | category | flops | bytes accessed | tf_op | source)
XLA Modules:
  0.0 147.3 jit_solution(3102041822106230282)
XLA Ops:
  0.7 0.6 copy-done.9
  1.3 4.8 %column_sums.1 = (f32[8,16,128]{2,1,0:T(8,128)S(1)}, bf16[48,128,128]{2,1,0:T(8,128)(2,1)}, bf16[16,128,128]{2,1,0:T(8,128)(2,1)}) custom-call(s32[64]{0:T(128)S(1)} %copy-done.9, s32[1]{0:T(128)} %copy.10.count, bf16[64,128,128]{2,1,0:T(8,128)(2,1)} %rest_8_.5), custom_call_target="tpu_custom_call" | custom-call | flops 1048576 | bytes 4194304 | tf_op jit(solution)/shard_map/column_sums/pallas_call | solution.py:61
  6.1 3.0 %collective-permute-start.14 = (bf16[48,128,128]{2,1,0:T(8,128)(2,1)}, bf16[48,128,128]{2,1,0:T(8,128)(2,1)}, u32[]{:S(2)}, u32[]{:S(2)}) collective-permute-start(bf16[48,128,128]{2,1,0:T(8,128)(2,1)} %get-tuple-element.37), channel_id=1, source_target_pairs={{0,2},{1,3},{2,0},{3,1},{4,6},{5,7},{6,4},{7,5},{8,10},{9,11},{10,... | collective-permute-start | bytes 4718600 | tf_op jit(solution)/shard_map/ppermute | solution.py:24
  9.1 15.1 %documents.1 = (f32[16,2176]{1,0:T(8,128)S(1)}, f32[16,2176]{1,0:T(8,128)S(1)}, f32[16,2176]{1,0:T(8,128)S(1)}, f32[16,2176]{1,0:T(8,128)S(1)}) custom-call(s32[1]{0:T(128)} %bitcast.1.place, bf16[8192,768]{1,0:T(8,128)(2,1)} %docs.1, bf16[768,256]{1,0:T(8,128)(2,1)S(1)} %copy-done.11, bf16[64,256]{1,0:T(8,128)(2,1)S(1)} %bitcast.12, ...), custom_call_target="tpu_custom_call" | custom-call | flops 7784628224 | bytes 12582912 | tf_op jit(solution)/shard_map/documents/pallas_call | solution.py:143
  24.3 0.6 collective-permute-start
  24.8 1.4 collective-permute-start.2
  26.3 21.2 %collective-permute-done.1.rest_2_ = f32[16,2176]{1,0:T(8,128)S(1)} collective-permute-done((f32[16,2176]{1,0:T(8,128)S(1)}, f32[16,2176]{1,0:T(8,128)S(1)}, u32[]{:S(2)}, u32[]{:S(2)}) %collective-permute-start.1) | collective-permute-done | bytes 139296 | tf_op jit(solution)/shard_map/ppermute | solution.py:24
  47.5 1.4 collective-permute-done.2.rest_3_
  48.9 0.6 collective-permute-start.16
  49.5 1.7 %collective-permute-start.15 = (bf16[16,128,128]{2,1,0:T(8,128)(2,1)}, bf16[16,128,128]{2,1,0:T(8,128)(2,1)S(1)}, u32[]{:S(2)}, u32[]{:S(2)}) collective-permute-start(bf16[16,128,128]{2,1,0:T(8,128)(2,1)} %get-tuple-element.39), channel_id=1, source_target_pairs={{0,2},{1,3},{2,0},{3,1},{4,6},{5,7},{6,4},{7,5},{8,10},{9,11},{10,... | collective-permute-start | bytes 1572872 | tf_op jit(solution)/shard_map/ppermute | solution.py:24
  51.2 12.5 %all_to_all.5 = f32[8,16,128]{2,1,0:T(8,128)S(1)} all-to-all(f32[8,16,128]{2,1,0:T(8,128)S(1)} %get-tuple-element.27), channel_id=1, replica_groups=mesh['hst'=8,'doc'=4] {'hst'}, dimensions={0} | all-to-all | bytes 131072 | tf_op jit(solution)/shard_map/all_to_all | solution.py:389
  63.8 0.6 collective-permute-start.4
  64.4 2.5 %collective-permute-done.5.rest_7_ = f32[16,128]{1,0:T(8,128)S(1)} collective-permute-done((f32[16,128]{1,0:T(8,128)S(1)}, f32[16,128]{1,0:T(8,128)S(1)}, u32[]{:S(2)}, u32[]{:S(2)}) %collective-permute-start.5) | collective-permute-done | bytes 8224 | tf_op jit(solution)/shard_map/ppermute | solution.py:24
  66.9 0.7 collective-permute-done.4.rest_6_
  67.5 0.5 collective-permute-done.3.rest_5_
  68.1 0.1 start_values.1
  68.2 0.7 collective-permute-start.11
  68.9 1.0 collective-permute-start.9
  69.9 5.2 %collective-permute-done.11.rest_6_ = bf16[16,2176]{1,0:T(8,128)(2,1)S(1)} collective-permute-done((bf16[16,2176]{1,0:T(8,128)(2,1)S(1)}, bf16[16,2176]{1,0:T(8,128)(2,1)S(1)}, u32[]{:S(2)}, u32[]{:S(2)}) %collective-permute-start.11) | collective-permute-done | bytes 69664 | tf_op jit(solution)/shard_map/ppermute | solution.py:24
  75.2 1.7 %collective-permute-done.9.rest_4_ = bf16[16,2176]{1,0:T(8,128)(2,1)S(1)} collective-permute-done((bf16[16,2176]{1,0:T(8,128)(2,1)S(1)}, bf16[16,2176]{1,0:T(8,128)(2,1)S(1)}, u32[]{:S(2)}, u32[]{:S(2)}) %collective-permute-start.9) | collective-permute-done | bytes 69664 | tf_op jit(solution)/shard_map/ppermute | solution.py:24
  76.8 1.0 collective-permute-start.6
  77.8 1.7 %collective-permute-done.7.rest_2_ = bf16[16,2176]{1,0:T(8,128)(2,1)S(1)} collective-permute-done((bf16[16,2176]{1,0:T(8,128)(2,1)S(1)}, bf16[16,2176]{1,0:T(8,128)(2,1)S(1)}, u32[]{:S(2)}, u32[]{:S(2)}) %collective-permute-start.7) | collective-permute-done | bytes 69664 | tf_op jit(solution)/shard_map/ppermute | solution.py:24
  79.5 0.4 collective-permute-start.10
  79.9 1.7 %collective-permute-done.6.rest_1_ = bf16[16,2176]{1,0:T(8,128)(2,1)S(1)} collective-permute-done((bf16[16,2176]{1,0:T(8,128)(2,1)S(1)}, bf16[16,2176]{1,0:T(8,128)(2,1)S(1)}, u32[]{:S(2)}, u32[]{:S(2)}) %collective-permute-start.6) | collective-permute-done | bytes 69664 | tf_op jit(solution)/shard_map/ppermute | solution.py:24
  81.5 0.6 copy-done.2
  82.2 1.0 collective-permute-start.8
  83.2 0.6 copy-done
  83.8 0.3 collective-permute-done.10.rest_5_
  84.2 0.6 copy-done.4
  84.8 1.7 %collective-permute-done.8.rest_3_ = bf16[16,2176]{1,0:T(8,128)(2,1)S(1)} collective-permute-done((bf16[16,2176]{1,0:T(8,128)(2,1)S(1)}, bf16[16,2176]{1,0:T(8,128)(2,1)S(1)}, u32[]{:S(2)}, u32[]{:S(2)}) %collective-permute-start.8) | collective-permute-done | bytes 69664 | tf_op jit(solution)/shard_map/ppermute | solution.py:24
  86.5 0.6 copy-done.6
  87.1 1.0 collective-permute-start.12
  88.1 0.1 pad_add_fusion.here
  88.2 3.5 %collective-permute-done.12.rest_7_ = bf16[16,2176]{1,0:T(8,128)(2,1)S(1)} collective-permute-done((bf16[16,2176]{1,0:T(8,128)(2,1)S(1)}, bf16[16,2176]{1,0:T(8,128)(2,1)S(1)}, u32[]{:S(2)}, u32[]{:S(2)}) %collective-permute-start.12) | collective-permute-done | bytes 69664 | tf_op jit(solution)/shard_map/ppermute | solution.py:24
  91.7 0.9 copy-done.1
  92.6 0.9 copy-done.3
  93.5 0.9 copy-done.5
  94.4 0.9 copy-done.7
  95.3 6.2 %hop.3 = (bf16[16,2048]{1,0:T(8,128)(2,1)S(1)}, f32[16,2048]{1,0:T(8,128)S(1)}) custom-call(s32[12,128]{1,0:T(8,128)S(1)} %get-tuple-element.34.meta, s32[2]{0:T(128)S(1)} %pad_add_fusion.here, bf16[16,2176]{1,0:T(8,128)(2,1)S(1)} %get-tuple-element.35.rest_0_, bf16[16,2176]{1,0:T(8,128)(2,1)S(1)} %copy-done.3, bf16[16,2176]{1,0:T(8,128)(2,1)S(1)} %copy-done.1, ...), custom_call_target="tpu_custom_call" | custom-call | flops 134217728 | bytes 8388608 | tf_op jit(solution)/shard_map/hop/pallas_call | solution.py:323
  101.4 2.3 %collective-permute-start.23 = (bf16[16,2048]{1,0:T(8,128)(2,1)S(1)}, bf16[16,2048]{1,0:T(8,128)(2,1)S(1)}, u32[]{:S(2)}, u32[]{:S(2)}) collective-permute-start(bf16[16,2048]{1,0:T(8,128)(2,1)S(1)} %get-tuple-element.43.rest_0_), channel_id=1, source_target_pairs={{0,24},{4,28},{8,16},{12,20},{16,8},{20,12},{24,0},{28,4},{1,25},{... | collective-permute-start | bytes 196616 | tf_op jit(solution)/shard_map/ppermute | solution.py:24
  103.7 2.2 %collective-permute-start.19 = (bf16[16,2048]{1,0:T(8,128)(2,1)S(1)}, bf16[16,2048]{1,0:T(8,128)(2,1)S(1)}, u32[]{:S(2)}, u32[]{:S(2)}) collective-permute-start(bf16[16,2048]{1,0:T(8,128)(2,1)S(1)} %get-tuple-element.43.rest_0_), channel_id=1, source_target_pairs={{0,8},{4,12},{8,0},{12,4},{16,24},{20,28},{24,16},{28,20},{1,9},{5... | collective-permute-start | bytes 196616 | tf_op jit(solution)/shard_map/ppermute | solution.py:24
  105.9 1.6 %collective-permute-start.18 = (bf16[16,2048]{1,0:T(8,128)(2,1)S(1)}, bf16[16,2048]{1,0:T(8,128)(2,1)S(1)}, u32[]{:S(2)}, u32[]{:S(2)}) collective-permute-start(bf16[16,2048]{1,0:T(8,128)(2,1)S(1)} %get-tuple-element.43.rest_0_), channel_id=1, source_target_pairs={{0,4},{4,0},{8,12},{12,8},{16,20},{20,16},{24,28},{28,24},{1,5},{5... | collective-permute-start | bytes 196616 | tf_op jit(solution)/shard_map/ppermute | solution.py:24
  107.4 0.4 collective-permute-done.23.rest_6_
  107.9 2.1 %collective-permute-start.24 = (bf16[16,2048]{1,0:T(8,128)(2,1)S(1)}, bf16[16,2048]{1,0:T(8,128)(2,1)S(1)}, u32[]{:S(2)}, u32[]{:S(2)}) collective-permute-start(bf16[16,2048]{1,0:T(8,128)(2,1)S(1)} %collective-permute-done.23.rest_6_), channel_id=1, source_target_pairs={{0,4},{4,0},{8,12},{12,8},{16,20},{20,16},{24,28},{28,24},{1,5},{5... | collective-permute-start | bytes 196616 | tf_op jit(solution)/shard_map/ppermute | solution.py:24
  109.9 1.4 collective-permute-start.22
  111.3 0.7 collective-permute-start.20
  112.0 0.2 collective-permute-done.24.rest_7_
  112.2 2.7 %collective-permute-done.22.rest_5_ = bf16[16,2048]{1,0:T(8,128)(2,1)S(1)} collective-permute-done((bf16[16,2048]{1,0:T(8,128)(2,1)S(1)}, bf16[16,2048]{1,0:T(8,128)(2,1)S(1)}, u32[]{:S(2)}, u32[]{:S(2)}) %collective-permute-start.22) | collective-permute-done | bytes 65568 | tf_op jit(solution)/shard_map/ppermute | solution.py:24
  114.9 0.7 collective-permute-done.20.rest_3_
  115.6 6.1 %hop.4.rest_0_ = bf16[16,2048]{1,0:T(8,128)(2,1)S(1)} custom-call(s32[12,128]{1,0:T(8,128)S(1)} %get-tuple-element.34.meta, s32[2]{0:T(128)S(1)} %pad_add_fusion.here, bf16[16,2048]{1,0:T(8,128)(2,1)S(1)} %get-tuple-element.43.rest_0_, bf16[16,2048]{1,0:T(8,128)(2,1)S(1)} %collective-permute-done.18.rest_1_, ...), custom_call_target="tpu_custom_call" | custom-call | flops 134217728 | bytes 8388608 | tf_op jit(solution)/shard_map/hop/pallas_call | solution.py:323
  121.7 2.6 %collective-permute-start.30 = (bf16[16,2048]{1,0:T(8,128)(2,1)S(1)}, bf16[16,2048]{1,0:T(8,128)(2,1)S(1)}, u32[]{:S(2)}, u32[]{:S(2)}) collective-permute-start(bf16[16,2048]{1,0:T(8,128)(2,1)S(1)} %hop.4.rest_0_), channel_id=1, source_target_pairs={{0,24},{4,28},{8,16},{12,20},{16,8},{20,12},{24,0},{28,4},{1,25},{... | collective-permute-start | bytes 196616 | tf_op jit(solution)/shard_map/ppermute | solution.py:24
  124.3 1.9 %collective-permute-start.26 = (bf16[16,2048]{1,0:T(8,128)(2,1)S(1)}, bf16[16,2048]{1,0:T(8,128)(2,1)S(1)}, u32[]{:S(2)}, u32[]{:S(2)}) collective-permute-start(bf16[16,2048]{1,0:T(8,128)(2,1)S(1)} %hop.4.rest_0_), channel_id=1, source_target_pairs={{0,8},{4,12},{8,0},{12,4},{16,24},{20,28},{24,16},{28,20},{1,9},{5... | collective-permute-start | bytes 196616 | tf_op jit(solution)/shard_map/ppermute | solution.py:24
  126.2 2.0 %collective-permute-start.25 = (bf16[16,2048]{1,0:T(8,128)(2,1)S(1)}, bf16[16,2048]{1,0:T(8,128)(2,1)S(1)}, u32[]{:S(2)}, u32[]{:S(2)}) collective-permute-start(bf16[16,2048]{1,0:T(8,128)(2,1)S(1)} %hop.4.rest_0_), channel_id=1, source_target_pairs={{0,4},{4,0},{8,12},{12,8},{16,20},{20,16},{24,28},{28,24},{1,5},{5... | collective-permute-start | bytes 196616 | tf_op jit(solution)/shard_map/ppermute | solution.py:24
  128.1 2.3 %collective-permute-start.31 = (bf16[16,2048]{1,0:T(8,128)(2,1)S(1)}, bf16[16,2048]{1,0:T(8,128)(2,1)S(1)}, u32[]{:S(2)}, u32[]{:S(2)}) collective-permute-start(bf16[16,2048]{1,0:T(8,128)(2,1)S(1)} %collective-permute-done.30.rest_6_), channel_id=1, source_target_pairs={{0,4},{4,0},{8,12},{12,8},{16,20},{20,16},{24,28},{28,24},{1,5},{5... | collective-permute-start | bytes 196616 | tf_op jit(solution)/shard_map/ppermute | solution.py:24
  130.5 2.0 %collective-permute-start.27 = (bf16[16,2048]{1,0:T(8,128)(2,1)S(1)}, bf16[16,2048]{1,0:T(8,128)(2,1)S(1)}, u32[]{:S(2)}, u32[]{:S(2)}) collective-permute-start(bf16[16,2048]{1,0:T(8,128)(2,1)S(1)} %collective-permute-done.26.rest_2_), channel_id=1, source_target_pairs={{0,4},{4,0},{8,12},{12,8},{16,20},{20,16},{24,28},{28,24},{1,5},{5... | collective-permute-start | bytes 196616 | tf_op jit(solution)/shard_map/ppermute | solution.py:24
  132.5 0.9 collective-permute-done.31.rest_7_
  133.4 1.3 collective-permute-done.29.rest_5_
  134.7 0.7 collective-permute-done.27.rest_3_
  135.4 6.1 %hop.5 = (f32[16,512]{1,0:T(8,128)S(1)}, f32[16,512]{1,0:T(8,128)S(1)}, f32[16,512]{1,0:T(8,128)S(1)}, f32[16,512]{1,0:T(8,128)S(1)}) custom-call(s32[12,128]{1,0:T(8,128)S(1)} %get-tuple-element.34.meta, s32[2]{0:T(128)S(1)} %pad_add_fusion.here, bf16[16,2048]{1,0:T(8,128)(2,1)S(1)} %hop.4.rest_0_, bf16[16,2048]{1,0:T(8,128)(2,1)S(1)} %collective-permute-done.25.rest_1_, ...), custom_call_target="tpu_custom_call" | custom-call | flops 134217728 | bytes 8388608 | tf_op jit(solution)/shard_map/hop/pallas_call | solution.py:323
  141.6 0.8 collective-permute-start.33
  142.4 1.1 collective-permute-start.34
  143.5 2.3 %collective-permute-done.33.rest_2_ = f32[16,512]{1,0:T(8,128)S(1)} collective-permute-done((f32[16,512]{1,0:T(8,128)S(1)}, f32[16,512]{1,0:T(8,128)S(1)}, u32[]{:S(2)}, u32[]{:S(2)}) %collective-permute-start.33) | collective-permute-done | bytes 32800 | tf_op jit(solution)/shard_map/ppermute | solution.py:24
  145.8 0.3 collective-permute-done.34.rest_3_
  146.1 1.2 finish.1
  (46 shorter events, 0.3 us)
Async XLA Ops:
  0.0 9.1 %copy-start.10 = (s32[64]{0:T(128)S(1)}, s32[64]{0:T(128)}, u32[]{:S(2)}) copy-start(s32[64]{0:T(128)} %source.1) | copy-start | bytes 772
  0.0 9.1 %copy-start.14 = (s32[64]{0:T(128)S(1)}, s32[64]{0:T(128)}, u32[]{:S(2)}) copy-start(s32[64]{0:T(128)} %param.14) | copy-start | bytes 772
  0.7 0.7 copy-start.9
  1.3 7.8 %copy-start.11 = (bf16[768,256]{1,0:T(8,128)(2,1)S(1)}, bf16[768,256]{1,0:T(8,128)(2,1)}, u32[]{:S(2)}) copy-start(bf16[768,256]{1,0:T(8,128)(2,1)} %w_in.1) | copy-start | bytes 1179652
  1.3 7.8 %copy-start.12 = (bf16[256,64]{0,1:T(8,128)(2,1)S(1)}, bf16[256,64]{0,1:T(8,128)(2,1)}, u32[]{:S(2)}) copy-start(bf16[256,64]{0,1:T(8,128)(2,1)} %param.11) | copy-start | bytes 98308
  1.3 7.8 %copy-start.13 = (s32[8192]{0:T(1024)S(1)}, s32[8192]{0:T(1024)}, u32[]{:S(2)}) copy-start(s32[8192]{0:T(1024)} %param.12) | copy-start | bytes 98308
  6.1 42.8 %collective-permute-start.14 = (bf16[48,128,128]{2,1,0:T(8,128)(2,1)}, bf16[48,128,128]{2,1,0:T(8,128)(2,1)}, u32[]{:S(2)}, u32[]{:S(2)}) collective-permute-start(bf16[48,128,128]{2,1,0:T(8,128)(2,1)} %get-tuple-element.37), channel_id=1, source_target_pairs={{0,2},{1,3},{2,0},{3,1},{4,6},{5,7},{6,4},{7,5},{8,10},{9,11},{10,... | collective-permute-start | bytes 4718600 | tf_op jit(solution)/shard_map/ppermute | solution.py:24
  9.1 82.6 %collective-permute-start.13 = (bf16[64,128,128]{2,1,0:T(8,128)(2,1)}, bf16[64,128,128]{2,1,0:T(8,128)(2,1)S(1)}, u32[]{:S(2)}, u32[]{:S(2)}) collective-permute-start(bf16[64,128,128]{2,1,0:T(8,128)(2,1)} %rest_8_.5), channel_id=1, source_target_pairs={{0,1},{1,0},{2,3},{3,2},{4,5},{5,4},{6,7},{7,6},{8,9},{9,8},{10,11... | collective-permute-start | bytes 6291464 | tf_op jit(solution)/shard_map/ppermute | solution.py:24
  9.1 58.9 %copy-start.8 = (s32[2048]{0:T(1024)S(1)}, s32[2048]{0:T(1024)}, u32[]{:S(2)}) copy-start(s32[2048]{0:T(1024)} %param.17) | copy-start | bytes 24580
  24.3 2.0 %collective-permute-start = (f32[16,2176]{1,0:T(8,128)S(1)}, f32[16,2176]{1,0:T(8,128)S(1)}, u32[]{:S(2)}, u32[]{:S(2)}) collective-permute-start(f32[16,2176]{1,0:T(8,128)S(1)} %get-tuple-element.30), channel_id=1, source_target_pairs={{0,1},{1,0},{2,3},{3,2},{4,5},{5,4},{6,7},{7,6},{8,9},{9,8},{10,11... | collective-permute-start | bytes 417800 | tf_op jit(solution)/shard_map/ppermute | solution.py:24
  24.8 22.7 %collective-permute-start.1 = (f32[16,2176]{1,0:T(8,128)S(1)}, f32[16,2176]{1,0:T(8,128)S(1)}, u32[]{:S(2)}, u32[]{:S(2)}) collective-permute-start(f32[16,2176]{1,0:T(8,128)S(1)} %get-tuple-element.31), channel_id=1, source_target_pairs={{0,2},{1,3},{2,0},{3,1},{4,6},{5,7},{6,4},{7,5},{8,10},{9,11},{10,... | collective-permute-start | bytes 417800 | tf_op jit(solution)/shard_map/ppermute | solution.py:24
  24.8 24.1 %collective-permute-start.2 = (f32[16,2176]{1,0:T(8,128)S(1)}, f32[16,2176]{1,0:T(8,128)S(1)}, u32[]{:S(2)}, u32[]{:S(2)}) collective-permute-start(f32[16,2176]{1,0:T(8,128)S(1)} %get-tuple-element.32), channel_id=1, source_target_pairs={{0,3},{1,2},{2,1},{3,0},{4,7},{5,6},{6,5},{7,4},{8,11},{9,10},{10,... | collective-permute-start | bytes 417800 | tf_op jit(solution)/shard_map/ppermute | solution.py:24
  48.9 42.8 %collective-permute-start.16 = (bf16[48,128,128]{2,1,0:T(8,128)(2,1)}, bf16[48,128,128]{2,1,0:T(8,128)(2,1)}, u32[]{:S(2)}, u32[]{:S(2)}) collective-permute-start(bf16[48,128,128]{2,1,0:T(8,128)(2,1)} %collective-permute-done.14.rest_10_), channel_id=1, source_target_pairs={{0,1},{1,0},{2,3},{3,2},{4,5},{5,4},{6,7},{7,6},{8,9},{9,8},{10,11... | collective-permute-start | bytes 4718600 | tf_op jit(solution)/shard_map/ppermute | solution.py:24
  49.5 37.6 %collective-permute-start.15 = (bf16[16,128,128]{2,1,0:T(8,128)(2,1)}, bf16[16,128,128]{2,1,0:T(8,128)(2,1)S(1)}, u32[]{:S(2)}, u32[]{:S(2)}) collective-permute-start(bf16[16,128,128]{2,1,0:T(8,128)(2,1)} %get-tuple-element.39), channel_id=1, source_target_pairs={{0,2},{1,3},{2,0},{3,1},{4,6},{5,7},{6,4},{7,5},{8,10},{9,11},{10,... | collective-permute-start | bytes 1572872 | tf_op jit(solution)/shard_map/ppermute | solution.py:24
  63.7 3.1 %collective-permute-start.5 = (f32[16,128]{1,0:T(8,128)S(1)}, f32[16,128]{1,0:T(8,128)S(1)}, u32[]{:S(2)}, u32[]{:S(2)}) collective-permute-start(f32[16,128]{1,0:T(8,128)S(1)} %reduce_sum.9.rest_4_), channel_id=1, source_target_pairs={{0,3},{1,2},{2,1},{3,0},{4,7},{5,6},{6,5},{7,4},{8,11},{9,10},{10,... | collective-permute-start | bytes 24584 | tf_op jit(solution)/shard_map/ppermute | solution.py:24
  63.8 3.7 %collective-permute-start.4 = (f32[16,128]{1,0:T(8,128)S(1)}, f32[16,128]{1,0:T(8,128)S(1)}, u32[]{:S(2)}, u32[]{:S(2)}) collective-permute-start(f32[16,128]{1,0:T(8,128)S(1)} %reduce_sum.9.rest_4_), channel_id=1, source_target_pairs={{0,2},{1,3},{2,0},{3,1},{4,6},{5,7},{6,4},{7,5},{8,10},{9,11},{10,... | collective-permute-start | bytes 24584 | tf_op jit(solution)/shard_map/ppermute | solution.py:24
  66.9 1.2 collective-permute-start.3
  68.2 7.0 %collective-permute-start.11 = (bf16[16,2176]{1,0:T(8,128)(2,1)S(1)}, bf16[16,2176]{1,0:T(8,128)(2,1)S(1)}, u32[]{:S(2)}, u32[]{:S(2)}) collective-permute-start(bf16[16,2176]{1,0:T(8,128)(2,1)S(1)} %get-tuple-element.35.rest_0_), channel_id=1, source_target_pairs={{0,24},{4,28},{8,16},{12,20},{16,8},{20,12},{24,0},{28,4},{1,25},{... | collective-permute-start | bytes 208904 | tf_op jit(solution)/shard_map/ppermute | solution.py:24
  68.9 8.0 %collective-permute-start.9 = (bf16[16,2176]{1,0:T(8,128)(2,1)S(1)}, bf16[16,2176]{1,0:T(8,128)(2,1)S(1)}, u32[]{:S(2)}, u32[]{:S(2)}) collective-permute-start(bf16[16,2176]{1,0:T(8,128)(2,1)S(1)} %get-tuple-element.35.rest_0_), channel_id=1, source_target_pairs={{0,16},{4,20},{8,24},{12,28},{16,0},{20,4},{24,8},{28,12},{1,17},{... | collective-permute-start | bytes 208904 | tf_op jit(solution)/shard_map/ppermute | solution.py:24
  75.2 4.3 %collective-permute-start.7 = (bf16[16,2176]{1,0:T(8,128)(2,1)S(1)}, bf16[16,2176]{1,0:T(8,128)(2,1)S(1)}, u32[]{:S(2)}, u32[]{:S(2)}) collective-permute-start(bf16[16,2176]{1,0:T(8,128)(2,1)S(1)} %get-tuple-element.35.rest_0_), channel_id=1, source_target_pairs={{0,8},{4,12},{8,0},{12,4},{16,24},{20,28},{24,16},{28,20},{1,9},{5... | collective-permute-start | bytes 208904 | tf_op jit(solution)/shard_map/ppermute | solution.py:24
  76.8 4.7 %collective-permute-start.6 = (bf16[16,2176]{1,0:T(8,128)(2,1)S(1)}, bf16[16,2176]{1,0:T(8,128)(2,1)S(1)}, u32[]{:S(2)}, u32[]{:S(2)}) collective-permute-start(bf16[16,2176]{1,0:T(8,128)(2,1)S(1)} %get-tuple-element.35.rest_0_), channel_id=1, source_target_pairs={{0,4},{4,0},{8,12},{12,8},{16,20},{20,16},{24,28},{28,24},{1,5},{5... | collective-permute-start | bytes 208904 | tf_op jit(solution)/shard_map/ppermute | solution.py:24
  79.5 4.7 %collective-permute-start.10 = (bf16[16,2176]{1,0:T(8,128)(2,1)S(1)}, bf16[16,2176]{1,0:T(8,128)(2,1)S(1)}, u32[]{:S(2)}, u32[]{:S(2)}) collective-permute-start(bf16[16,2176]{1,0:T(8,128)(2,1)S(1)} %collective-permute-done.9.rest_4_), channel_id=1, source_target_pairs={{0,4},{4,0},{8,12},{12,8},{16,20},{20,16},{24,28},{28,24},{1,5},{5... | collective-permute-start | bytes 208904 | tf_op jit(solution)/shard_map/ppermute | solution.py:24
  81.5 0.6 copy-start.2
  82.2 4.3 %collective-permute-start.8 = (bf16[16,2176]{1,0:T(8,128)(2,1)S(1)}, bf16[16,2176]{1,0:T(8,128)(2,1)S(1)}, u32[]{:S(2)}, u32[]{:S(2)}) collective-permute-start(bf16[16,2176]{1,0:T(8,128)(2,1)S(1)} %collective-permute-done.7.rest_2_), channel_id=1, source_target_pairs={{0,4},{4,0},{8,12},{12,8},{16,20},{20,16},{24,28},{28,24},{1,5},{5... | collective-permute-start | bytes 208904 | tf_op jit(solution)/shard_map/ppermute | solution.py:24
  83.2 0.6 copy-start
  84.2 0.6 copy-start.4
  86.5 0.6 copy-start.6
  87.1 4.6 %collective-permute-start.17 = (bf16[16,128,128]{2,1,0:T(8,128)(2,1)S(1)}, bf16[16,128,128]{2,1,0:T(8,128)(2,1)S(1)}, u32[]{:S(2)}, u32[]{:S(2)}) collective-permute-start(bf16[16,128,128]{2,1,0:T(8,128)(2,1)S(1)} %collective-permute-done.15.rest_11_), channel_id=1, source_target_pairs={{0,1},{1,0},{2,3},{3,2},{4,5},{5,4},{6,7},{7,6},{8,9},{9,8},{10,11... | collective-permute-start | bytes 1572872 | tf_op jit(solution)/shard_map/ppermute | solution.py:24
  87.1 4.6 %collective-permute-start.12 = (bf16[16,2176]{1,0:T(8,128)(2,1)S(1)}, bf16[16,2176]{1,0:T(8,128)(2,1)S(1)}, u32[]{:S(2)}, u32[]{:S(2)}) collective-permute-start(bf16[16,2176]{1,0:T(8,128)(2,1)S(1)} %collective-permute-done.11.rest_6_), channel_id=1, source_target_pairs={{0,4},{4,0},{8,12},{12,8},{16,20},{20,16},{24,28},{28,24},{1,5},{5... | collective-permute-start | bytes 208904 | tf_op jit(solution)/shard_map/ppermute | solution.py:24
  91.7 0.9 copy-start.1
  92.6 0.9 copy-start.3
  93.5 0.9 copy-start.5
  94.4 0.9 copy-start.7
  101.4 6.4 %collective-permute-start.23 = (bf16[16,2048]{1,0:T(8,128)(2,1)S(1)}, bf16[16,2048]{1,0:T(8,128)(2,1)S(1)}, u32[]{:S(2)}, u32[]{:S(2)}) collective-permute-start(bf16[16,2048]{1,0:T(8,128)(2,1)S(1)} %get-tuple-element.43.rest_0_), channel_id=1, source_target_pairs={{0,24},{4,28},{8,16},{12,20},{16,8},{20,12},{24,0},{28,4},{1,25},{... | collective-permute-start | bytes 196616 | tf_op jit(solution)/shard_map/ppermute | solution.py:24
  103.7 6.2 %collective-permute-start.21 = (bf16[16,2048]{1,0:T(8,128)(2,1)S(1)}, bf16[16,2048]{1,0:T(8,128)(2,1)S(1)}, u32[]{:S(2)}, u32[]{:S(2)}) collective-permute-start(bf16[16,2048]{1,0:T(8,128)(2,1)S(1)} %get-tuple-element.43.rest_0_), channel_id=1, source_target_pairs={{0,16},{4,20},{8,24},{12,28},{16,0},{20,4},{24,8},{28,12},{1,17},{... | collective-permute-start | bytes 196616 | tf_op jit(solution)/shard_map/ppermute | solution.py:24
  103.7 7.6 %collective-permute-start.19 = (bf16[16,2048]{1,0:T(8,128)(2,1)S(1)}, bf16[16,2048]{1,0:T(8,128)(2,1)S(1)}, u32[]{:S(2)}, u32[]{:S(2)}) collective-permute-start(bf16[16,2048]{1,0:T(8,128)(2,1)S(1)} %get-tuple-element.43.rest_0_), channel_id=1, source_target_pairs={{0,8},{4,12},{8,0},{12,4},{16,24},{20,28},{24,16},{28,20},{1,9},{5... | collective-permute-start | bytes 196616 | tf_op jit(solution)/shard_map/ppermute | solution.py:24
  105.9 6.1 %collective-permute-start.18 = (bf16[16,2048]{1,0:T(8,128)(2,1)S(1)}, bf16[16,2048]{1,0:T(8,128)(2,1)S(1)}, u32[]{:S(2)}, u32[]{:S(2)}) collective-permute-start(bf16[16,2048]{1,0:T(8,128)(2,1)S(1)} %get-tuple-element.43.rest_0_), channel_id=1, source_target_pairs={{0,4},{4,0},{8,12},{12,8},{16,20},{20,16},{24,28},{28,24},{1,5},{5... | collective-permute-start | bytes 196616 | tf_op jit(solution)/shard_map/ppermute | solution.py:24
  107.9 4.3 %collective-permute-start.24 = (bf16[16,2048]{1,0:T(8,128)(2,1)S(1)}, bf16[16,2048]{1,0:T(8,128)(2,1)S(1)}, u32[]{:S(2)}, u32[]{:S(2)}) collective-permute-start(bf16[16,2048]{1,0:T(8,128)(2,1)S(1)} %collective-permute-done.23.rest_6_), channel_id=1, source_target_pairs={{0,4},{4,0},{8,12},{12,8},{16,20},{20,16},{24,28},{28,24},{1,5},{5... | collective-permute-start | bytes 196616 | tf_op jit(solution)/shard_map/ppermute | solution.py:24
  109.9 4.9 %collective-permute-start.22 = (bf16[16,2048]{1,0:T(8,128)(2,1)S(1)}, bf16[16,2048]{1,0:T(8,128)(2,1)S(1)}, u32[]{:S(2)}, u32[]{:S(2)}) collective-permute-start(bf16[16,2048]{1,0:T(8,128)(2,1)S(1)} %collective-permute-done.21.rest_4_), channel_id=1, source_target_pairs={{0,4},{4,0},{8,12},{12,8},{16,20},{20,16},{24,28},{28,24},{1,5},{5... | collective-permute-start | bytes 196616 | tf_op jit(solution)/shard_map/ppermute | solution.py:24
  111.3 4.3 %collective-permute-start.20 = (bf16[16,2048]{1,0:T(8,128)(2,1)S(1)}, bf16[16,2048]{1,0:T(8,128)(2,1)S(1)}, u32[]{:S(2)}, u32[]{:S(2)}) collective-permute-start(bf16[16,2048]{1,0:T(8,128)(2,1)S(1)} %collective-permute-done.19.rest_2_), channel_id=1, source_target_pairs={{0,4},{4,0},{8,12},{12,8},{16,20},{20,16},{24,28},{28,24},{1,5},{5... | collective-permute-start | bytes 196616 | tf_op jit(solution)/shard_map/ppermute | solution.py:24
  121.7 6.4 %collective-permute-start.30 = (bf16[16,2048]{1,0:T(8,128)(2,1)S(1)}, bf16[16,2048]{1,0:T(8,128)(2,1)S(1)}, u32[]{:S(2)}, u32[]{:S(2)}) collective-permute-start(bf16[16,2048]{1,0:T(8,128)(2,1)S(1)} %hop.4.rest_0_), channel_id=1, source_target_pairs={{0,24},{4,28},{8,16},{12,20},{16,8},{20,12},{24,0},{28,4},{1,25},{... | collective-permute-start | bytes 196616 | tf_op jit(solution)/shard_map/ppermute | solution.py:24
  124.3 6.2 %collective-permute-start.28 = (bf16[16,2048]{1,0:T(8,128)(2,1)S(1)}, bf16[16,2048]{1,0:T(8,128)(2,1)S(1)}, u32[]{:S(2)}, u32[]{:S(2)}) collective-permute-start(bf16[16,2048]{1,0:T(8,128)(2,1)S(1)} %hop.4.rest_0_), channel_id=1, source_target_pairs={{0,16},{4,20},{8,24},{12,28},{16,0},{20,4},{24,8},{28,12},{1,17},{... | collective-permute-start | bytes 196616 | tf_op jit(solution)/shard_map/ppermute | solution.py:24
  124.3 6.2 %collective-permute-start.26 = (bf16[16,2048]{1,0:T(8,128)(2,1)S(1)}, bf16[16,2048]{1,0:T(8,128)(2,1)S(1)}, u32[]{:S(2)}, u32[]{:S(2)}) collective-permute-start(bf16[16,2048]{1,0:T(8,128)(2,1)S(1)} %hop.4.rest_0_), channel_id=1, source_target_pairs={{0,8},{4,12},{8,0},{12,4},{16,24},{20,28},{24,16},{28,20},{1,9},{5... | collective-permute-start | bytes 196616 | tf_op jit(solution)/shard_map/ppermute | solution.py:24
  126.2 6.3 %collective-permute-start.25 = (bf16[16,2048]{1,0:T(8,128)(2,1)S(1)}, bf16[16,2048]{1,0:T(8,128)(2,1)S(1)}, u32[]{:S(2)}, u32[]{:S(2)}) collective-permute-start(bf16[16,2048]{1,0:T(8,128)(2,1)S(1)} %hop.4.rest_0_), channel_id=1, source_target_pairs={{0,4},{4,0},{8,12},{12,8},{16,20},{20,16},{24,28},{28,24},{1,5},{5... | collective-permute-start | bytes 196616 | tf_op jit(solution)/shard_map/ppermute | solution.py:24
  128.1 5.3 %collective-permute-start.31 = (bf16[16,2048]{1,0:T(8,128)(2,1)S(1)}, bf16[16,2048]{1,0:T(8,128)(2,1)S(1)}, u32[]{:S(2)}, u32[]{:S(2)}) collective-permute-start(bf16[16,2048]{1,0:T(8,128)(2,1)S(1)} %collective-permute-done.30.rest_6_), channel_id=1, source_target_pairs={{0,4},{4,0},{8,12},{12,8},{16,20},{20,16},{24,28},{28,24},{1,5},{5... | collective-permute-start | bytes 196616 | tf_op jit(solution)/shard_map/ppermute | solution.py:24
  130.5 4.3 %collective-permute-start.29 = (bf16[16,2048]{1,0:T(8,128)(2,1)S(1)}, bf16[16,2048]{1,0:T(8,128)(2,1)S(1)}, u32[]{:S(2)}, u32[]{:S(2)}) collective-permute-start(bf16[16,2048]{1,0:T(8,128)(2,1)S(1)} %collective-permute-done.28.rest_4_), channel_id=1, source_target_pairs={{0,4},{4,0},{8,12},{12,8},{16,20},{20,16},{24,28},{28,24},{1,5},{5... | collective-permute-start | bytes 196616 | tf_op jit(solution)/shard_map/ppermute | solution.py:24
  130.5 4.9 %collective-permute-start.27 = (bf16[16,2048]{1,0:T(8,128)(2,1)S(1)}, bf16[16,2048]{1,0:T(8,128)(2,1)S(1)}, u32[]{:S(2)}, u32[]{:S(2)}) collective-permute-start(bf16[16,2048]{1,0:T(8,128)(2,1)S(1)} %collective-permute-done.26.rest_2_), channel_id=1, source_target_pairs={{0,4},{4,0},{8,12},{12,8},{16,20},{20,16},{24,28},{28,24},{1,5},{5... | collective-permute-start | bytes 196616 | tf_op jit(solution)/shard_map/ppermute | solution.py:24
  141.5 1.9 %collective-permute-start.32 = (f32[16,512]{1,0:T(8,128)S(1)}, f32[16,512]{1,0:T(8,128)S(1)}, u32[]{:S(2)}, u32[]{:S(2)}) collective-permute-start(f32[16,512]{1,0:T(8,128)S(1)} %get-tuple-element.46), channel_id=1, source_target_pairs={{0,1},{1,0},{2,3},{3,2},{4,5},{5,4},{6,7},{7,6},{8,9},{9,8},{10,11... | collective-permute-start | bytes 98312 | tf_op jit(solution)/shard_map/ppermute | solution.py:24
  141.6 4.2 %collective-permute-start.33 = (f32[16,512]{1,0:T(8,128)S(1)}, f32[16,512]{1,0:T(8,128)S(1)}, u32[]{:S(2)}, u32[]{:S(2)}) collective-permute-start(f32[16,512]{1,0:T(8,128)S(1)} %get-tuple-element.47), channel_id=1, source_target_pairs={{0,2},{1,3},{2,0},{3,1},{4,6},{5,7},{6,4},{7,5},{8,10},{9,11},{10,... | collective-permute-start | bytes 98312 | tf_op jit(solution)/shard_map/ppermute | solution.py:24
  142.4 3.7 %collective-permute-start.34 = (f32[16,512]{1,0:T(8,128)S(1)}, f32[16,512]{1,0:T(8,128)S(1)}, u32[]{:S(2)}, u32[]{:S(2)}) collective-permute-start(f32[16,512]{1,0:T(8,128)S(1)} %get-tuple-element.48), channel_id=1, source_target_pairs={{0,3},{1,2},{2,1},{3,0},{4,7},{5,6},{6,5},{7,4},{8,11},{9,10},{10,... | collective-permute-start | bytes 98312 | tf_op jit(solution)/shard_map/ppermute | solution.py:24
